TPU v7x, 32 devices: a whole 2x2x4 slice. The times are simulated.
32 devices in a mesh: row: 4 (over y, x), col: 8 (over z, core).
Axes of the slice: x: 2, y: 2, z: 4, core: 2. Of those that a mesh axis runs over, the one named last changes fastest.
Arguments:
- amplitude: float32 [800, 20480], P('row', 'col'), may hold values from -6 to 6
- ladder_coupling: float32 [20480, 20480], P('row', 'col'), may hold values from -0.0390625 to 0.0390625
- crossed_coupling: float32 [4, 1280, 1280], P('row'), may hold values from -0.15625 to 0.15625
- channel_slot: int32 [4], replicated, may hold values from 0 to 3, each once
- channel_of: int32 [8, 512, 1], P('col', 'row'), may hold values from 0 to 3; in each aligned block of 128 rows (0 to 127, 128 to 255, ..., all dimensions but the last counted through in order) at most 40 rows name the same one
- source_row: int32 [8, 512], P('col', 'row'), may hold values from 0 to 1599
- target_row: int32 [8, 512], P('col', 'row'), may hold values from 0 to 3199
- recoupling: float32 [8, 512], P('col', 'row'), may hold values from -1 to 1
- driving: float32 [800, 20480], P('col', 'row'), may hold values from -6 to 6
- denominator: float32 [800, 20480], P('col', 'row'), may hold values from 1 to 10
Outputs:
- updated: float32 [800, 20480], P('col', 'row')
Inputs may be any that keep to these rules, and one draw needn't show every extreme that they name: Among the 128 segments of one device (aligned blocks of channel_of's rows), no channel is named more than 40 times; some channel is named exactly 40 times in some device's segments. `channel_slot`: each slot once.
All inputs are finite; a program needn't handle non-finite values.
Results may differ from a plain program's by a relative error of at most 0.0003.
Values sent between devices are 32-bit elements; how exact they have to be, the bound alone decides.
No kernel may reach another device: no remote copies, remote signals or barrier semaphores. Data moves between devices by JAX's collectives and lax.ppermute only.
A program may use at most 192 MiB of HBM per device.

v0:
```python
import jax
import jax.numpy as jnp
from jax import lax
from jax.sharding import PartitionSpec as P

CAP = 40


def on_device(
    amplitude,
    ladder_coupling,
    crossed_coupling,
    channel_slot,
    channel_of,
    source_row,
    target_row,
    recoupling,
    driving,
    denominator,
):
    highest = lax.Precision.HIGHEST
    gathered = lax.all_gather(amplitude, "row", axis=0, tiled=True)
    hole_pairs = gathered.shape[0]
    segment_width = crossed_coupling.shape[1]
    row_width = ladder_coupling.shape[0]
    groups = lax.axis_size("row")
    capacity = CAP
    flat_rows = gathered.reshape(-1, segment_width)
    picked = flat_rows[source_row[0]] * recoupling[0][:, None]
    owners = channel_slot[channel_of[0, :, 0]]
    onehot = (owners[:, None] == jnp.arange(groups, dtype=jnp.int32)[None, :]).astype(jnp.int32)
    before = jnp.cumsum(onehot, axis=0) - onehot
    placed = jnp.sum(before * onehot, axis=1)
    target = owners * capacity + placed
    buffer = jnp.zeros((groups * capacity, segment_width), jnp.float32).at[target].set(picked)
    buffer = buffer.reshape(groups, capacity, segment_width)
    mixture = jnp.einsum(
        "plf,fm->plm",
        lax.all_to_all(buffer, "row", split_axis=0, concat_axis=0, tiled=True),
        crossed_coupling[0],
        precision=highest,
        preferred_element_type=jnp.float32,
    )
    returned = lax.all_to_all(mixture, "row", split_axis=0, concat_axis=0, tiled=True)
    back_rows = returned.reshape(groups * capacity, segment_width)[target]
    spread = (
        jnp.zeros((hole_pairs * (row_width // segment_width), segment_width), jnp.float32)
        .at[target_row[0]]
        .add(back_rows)
    )
    particle_hole = spread.reshape(hole_pairs, row_width)
    partial_value = (
        lax.dot_general(
            gathered,
            ladder_coupling,
            (((1,), (1,)), ((), ())),
            precision=highest,
            preferred_element_type=jnp.float32,
        )
        + particle_hole
    )
    summed = lax.psum_scatter(partial_value, "col", scatter_dimension=0, tiled=True)
    return (driving + summed) / denominator


def solution(mesh):
    in_specs = (
        P("row", "col"),
        P("row", "col"),
        P("row", None, None),
        P(),
        P("col", "row", None),
        P("col", "row"),
        P("col", "row"),
        P("col", "row"),
        P("col", "row"),
        P("col", "row"),
    )
    out_specs = P("col", "row")
    return jax.shard_map(
        on_device, mesh=mesh, in_specs=in_specs, out_specs=out_specs, check_vma=False
    )
```

profile of v0, /device:TPU:21, one launch (start us, length us, event | category | flops | bytes accessed | tf_op | source)
XLA Modules:
  0.0 505.0 jit_solution(8040035567016666543)
XLA Ops:
  6.5 0.0 all-gather.2.cloned.1.call-start
  6.5 0.7 all-gather.2.cloned.1.call-update
  7.3 1.4 fusion.17
  8.7 3.2 fusion.12
  11.9 0.1 fusion.11
  12.0 0.2 reduce_window_sum.11
  12.1 0.7 fusion.15
  12.8 0.2 select_reduce_fusion
  13.0 3.2 fusion.14
  16.2 0.0 copy-start
  16.2 80.1 %all-gather.2.cloned.1.call-done = f32[800,2560]{1,0:T(8,128)} async-done(((f32[200,2560]{1,0:T(8,128)}), f32[800,2560]{1,0:T(8,128)}) %all-gather.2.cloned.1.call-update) | async-done | bytes 8192016 | tf_op jit(solution)/shard_map/all_gather | solution.py:22
  96.2 9.3 %reshape.124 = f32[1600,1280]{1,0:T(8,128)} reshape(f32[800,2560]{1,0:T(8,128)} %all-gather.2.cloned.1.call-done) | data formatting | bytes 16384000 | tf_op jit(solution)/shard_map/reshape | solution.py:28
  105.6 0.0 copy-done
  105.6 0.0 copy-start.2
  105.6 3.1 scatter_custom_fusion
  108.7 12.8 %all_to_all.10 = f32[4,40,1280]{2,1,0:T(8,128)S(1)} all-to-all(f32[4,40,1280]{2,1,0:T(8,128)S(1)} %bitcast.37), channel_id=1, replica_groups=mesh['row'=4,'col'=8] {'row'}, dimensions={0} | all-to-all | bytes 1638400 | tf_op jit(solution)/shard_map/all_to_all | solution.py:39
  121.5 7.6 %fusion.3 = f32[4,40,1280]{2,1,0:T(8,128)} fusion(f32[4,40,1280]{2,1,0:T(8,128)S(1)} %all_to_all.10, f32[1,1280,1280]{2,1,0:T(8,128)} %param.12), kind=kOutput, calls=%fused_computation.7 | convolution fusion | flops 3145728000 | bytes 8192000 | tf_op jit(solution)/shard_map/plf,fm->plm/dot_general | solution.py:37
  129.1 4.5 all-to-all-start.1
  133.6 0.0 copy-done.2
  133.6 9.1 %all-to-all-done.1 = f32[4,40,1280]{2,1,0:T(8,128)S(1)} async-done(((f32[4,40,1280]{2,1,0:T(8,128)}), f32[4,40,1280]{2,1,0:T(8,128)S(1)}, u32[]{:S(2)}, u32[]{:S(2)}) %all-to-all-start.1) | async-done | bytes 819232 | tf_op jit(solution)/shard_map/all_to_all | solution.py:44
  142.7 9.1 %scatter_custom_fusion.1 = f32[3200,1280]{1,0:T(8,128)} fusion(s32[128]{0:T(128)S(1)} %fusion.13, f32[]{:T(128)} %constant.7.clone.1, f32[160,1280]{1,0:T(8,128)S(1)} %bitcast.38, s32[1024]{0:T(1024)S(1)} %pad_clamp_fusion), kind=kCustom, calls=%fused_computation.5 | custom fusion | flops 163840 | bytes 16384004 | tf_op jit(solution)/shard_map/scatter-add | solution.py:49
  151.8 18.3 %reshape.127 = f32[800,5120]{1,0:T(8,128)} reshape(f32[3200,1280]{1,0:T(8,128)} %scatter_custom_fusion.1) | data formatting | bytes 32768000 | tf_op jit(solution)/shard_map/reshape | solution.py:51
  170.1 135.9 %convolution_add_fusion = f32[800,5120]{1,0:T(8,128)} fusion(f32[800,5120]{1,0:T(8,128)} %reshape.127, f32[800,2560]{1,0:T(8,128)} %all-gather.2.cloned.1.call-done, f32[5120,2560]{1,0:T(8,128)} %param.11), kind=kOutput, calls=%fused_computation.4 | convolution fusion | flops 125833216000 | bytes 93388800 | tf_op jit(solution)/shard_map/dot_general | solution.py:53
  306.0 0.0 copy-start.1
  306.0 168.2 %fusion = f32[104,5120]{1,0:T(8,128)S(1)} fusion(f32[800,5120]{1,0:T(8,128)} %convolution_add_fusion), kind=kCustom, calls=%all-reduce-scatter | all-reduce-scatter fusion | flops 4259841 | bytes 18514432
  474.2 0.1 slice.9
  474.2 4.4 collective-permute-start
  478.6 0.0 copy-done.1
  478.6 0.6 dynamic-slice.4
  479.9 6.3 %collective-permute-done = f32[28,5120]{1,0:T(8,128)S(1)} collective-permute-done((f32[28,5120]{1,0:T(8,128)S(1)}, f32[28,5120]{1,0:T(8,128)S(1)}, u32[]{:S(2)}, u32[]{:S(2)}) %collective-permute-start) | collective-permute-done | bytes 573472
  486.1 7.4 %concatenate = f32[132,5120]{1,0:T(8,128)} concatenate(f32[28,5120]{1,0:T(8,128)S(1)} %collective-permute-done, f32[104,5120]{1,0:T(8,128)S(1)} %fusion), dimensions={0} | concatenate | bytes 5406720
  493.5 4.7 fusion.5
  (3 shorter events, 0.0 us)
Async XLA Ops:
  6.5 89.7 %all-gather.2.cloned.1.call-start = ((), (), s32[]{:S(2)}) async-start(), calls=%async_computation.2 | async-start | bytes 10240000 | tf_op jit(solution)/shard_map/all_gather | solution.py:22
  16.2 89.4 %copy-start = (f32[1,128]{1,0:T(1,128)S(1)}, f32[1,128]{1,0:T(1,128)}, u32[]{:S(2)}) copy-start(f32[1,128]{1,0:T(1,128)} %param.17) | copy-start | bytes 1540
  105.6 28.0 %copy-start.2 = (s32[1,128]{1,0:T(1,128)S(1)}, s32[1,128]{1,0:T(1,128)}, u32[]{:S(2)}) copy-start(s32[1,128]{1,0:T(1,128)} %param.16) | copy-start | bytes 1540
  129.1 13.6 %all-to-all-start.1 = ((f32[4,40,1280]{2,1,0:T(8,128)}), f32[4,40,1280]{2,1,0:T(8,128)S(1)}, u32[]{:S(2)}, u32[]{:S(2)}) async-start(f32[4,40,1280]{2,1,0:T(8,128)} %fusion.3), calls=%async_computation.1 | async-start | bytes 1638400 | tf_op jit(solution)/shard_map/all_to_all | solution.py:44
  306.0 172.7 %copy-start.1 = (u32[32]{0:T(128)S(1)}, u32[32]{0:T(128)}, u32[]{:S(2)}) copy-start(u32[32]{0:T(128)} %constant.33) | copy-start | bytes 388
  474.2 11.9 %collective-permute-start = (f32[28,5120]{1,0:T(8,128)S(1)}, f32[28,5120]{1,0:T(8,128)S(1)}, u32[]{:S(2)}, u32[]{:S(2)}) collective-permute-start(f32[28,5120]{1,0:T(8,128)S(1)} %slice.9), channel_id=1, source_target_pairs={{0,1},{1,2},{2,3},{3,4},{4,5},{5,6},{6,7},{8,9},{9,10},{10,11},{11... | collective-permute-start | bytes 1720328
Sparse Core Ops, SparseCore 0:
  9.2 86.9 all-gather.1
where the time goes:
time: 508 us; the launch traced here: 505 us
  blocking collectives  181 us (36%)
  matrix products  143 us (28%)
  waiting for transfers between devices  96.2 us (19%)
  local copies, waits for them, and re-layouts  37 us (7%)
  other arithmetic  24.4 us (5%)
  between operations  14.1 us (3%)
  starting transfers between devices  8.86 us (2%)
    unnamed x1, blocking collectives  168 us
    dot_general x1, matrix products, on_device(): lax.dot_general(gathered, ladder_coupling, (((1,), (1,)), ((), ())), prec...  136 us
    all_gather x1, waiting for transfers between devices, on_device(): gathered = lax.all_gather(amplitude, 'row', axis=0, tiled=True)  80.1 us
    reshape x1, local copies, waits for them, and re-layouts, on_device(): particle_hole = spread.reshape(hole_pairs, row_width)  18.3 us
    all_to_all x1, blocking collectives, on_device(): lax.all_to_all(buffer, 'row', split_axis=0, concat_axis=0, tiled=True)  12.8 us
  transfers between devices with their start and end apart: 3, of which 3 were waited for; matrix products, arithmetic and copies ran while one was open for 2% of the time, Pallas kernels for 0%

commit v1 on v0

v1 whole, which is shorter than its diff:
```python
import functools

import jax
import jax.numpy as jnp
from jax import lax
from jax.experimental import pallas as pl
from jax.experimental.pallas import tpu as pltpu
from jax.sharding import PartitionSpec as P

CAP = 40
F32 = jnp.float32
BF16 = jnp.bfloat16
VMEM_LIMIT = 56 * 1024 * 1024


def chunk_sizes(total):
    sizes = [32, 32, 36]
    return sizes if sum(sizes) == total else [24, total - 24]


def halves(x):
    high = x.astype(BF16)
    return high, (x - high.astype(F32)).astype(BF16)


def dot(x, y, contract):
    return lax.dot_general(x, y, ((contract[0], contract[1]), ((), ())), preferred_element_type=F32)


def ladder_kernel(n_pieces, where_ref, *refs):
    pieces = refs[:n_pieces]
    coupling_ref, *received, out_ref, amplitude_ref = refs[n_pieces:]
    groups, rows = out_ref.shape[:2]
    total = groups * rows
    gap = amplitude_ref.shape[1] // 2

    @pl.when(pl.program_id(0) == 0)
    def _():
        high, low = halves(jnp.concatenate([piece[...] for piece in pieces], axis=0).T)
        amplitude_ref[:, :total] = high
        amplitude_ref[:, gap : gap + total] = low

    coupling_high, coupling_low = halves(coupling_ref[...])
    nn = ((1,), (0,))
    both = dot(coupling_high, amplitude_ref[...], nn)
    value = both[:, :total] + both[:, gap : gap + total] + dot(coupling_low, amplitude_ref[:, :total], nn)
    value = value.T
    for k in range(groups):
        piece = value[k * rows : (k + 1) * rows]
        line = k ^ where_ref[0]
        out_ref[line] = piece + received[0][line] if received else piece


def ladder(where, pieces, coupling, width, received=None):
    rows, inner = pieces[0].shape
    total = sum(piece.shape[0] for piece in pieces)
    groups = total // rows
    part = width // 2
    segments = coupling.shape[0] // width
    block = pl.BlockSpec((groups, rows, part), lambda i, where: (0, 0, i))
    extra = [] if received is None else [received]
    return pl.pallas_call(
        functools.partial(ladder_kernel, len(pieces)),
        grid_spec=pltpu.PrefetchScalarGridSpec(
            num_scalar_prefetch=1,
            grid=(segments,),
            in_specs=[pl.BlockSpec(piece.shape, lambda i, where: (0, 0)) for piece in pieces]
            + [pl.BlockSpec((part, inner), lambda i, where: (2 * i + where[1], 0))]
            + [block] * len(extra),
            out_specs=block,
            scratch_shapes=[pltpu.VMEM((inner, 2 * (-(-total // 128) * 128)), BF16)],
        ),
        out_shape=jax.ShapeDtypeStruct((groups, rows, segments * part), F32),
        compiler_params=pltpu.CompilerParams(vmem_limit_bytes=VMEM_LIMIT),
        cost_estimate=pl.CostEstimate(
            flops=total * inner * segments * part,
            bytes_accessed=part * inner,
            transcendentals=0,
        ),
        name="ladder",
    )(where, *pieces, coupling, *extra)


def pick_kernel(counts, place_ref, segment_ref, factor_ref, *refs):
    pieces, out_ref = refs[:-1], refs[-1]
    slots = place_ref.shape[0]
    width = out_ref.shape[-1]
    picked = jnp.zeros((slots, pieces[0].shape[1]), F32)
    base = 0
    first = 0
    for number in counts:
        block = jnp.concatenate([piece[...] for piece in pieces[first : first + number]], axis=0)
        first += number
        high, low = halves(block)
        lanes = lax.broadcasted_iota(jnp.int32, (slots, block.shape[0]), 1) + base
        chosen = jnp.where(lanes == place_ref[...], 1.0, 0.0).astype(BF16)
        nn = ((1,), (0,))
        picked += dot(chosen, high, nn) + dot(chosen, low, nn)
        base += block.shape[0]
    value = picked[:, :width]
    for segment in range(1, picked.shape[1] // width):
        value = jnp.where(segment_ref[...] == segment, picked[:, segment * width : (segment + 1) * width], value)
    out_ref[...] = (value * factor_ref[...]).reshape(out_ref.shape)


def pick(place, segment, factor, chunks, groups, width):
    pieces = [piece for chunk in chunks for piece in chunk]
    slots = place.shape[0]
    return pl.pallas_call(
        functools.partial(pick_kernel, [len(chunk) for chunk in chunks]),
        out_shape=jax.ShapeDtypeStruct((groups, slots // groups, width), F32),
        compiler_params=pltpu.CompilerParams(vmem_limit_bytes=VMEM_LIMIT),
        cost_estimate=pl.CostEstimate(flops=slots * width, bytes_accessed=slots * width, transcendentals=0),
        name="pick",
    )(place, segment, factor, *pieces)


def mix_kernel(matrix_ref, *refs):
    pieces, out_ref = refs[:-1], refs[-1]
    high, low = halves(jnp.concatenate([piece[...] for piece in pieces], axis=0))
    matrix_high, matrix_low = halves(matrix_ref[...])
    nn = ((1,), (0,))
    value = dot(high, matrix_high, nn)
    value += dot(low, matrix_high, nn) + dot(high, matrix_low, nn)
    out_ref[...] = value.reshape(out_ref.shape)


def mix(matrix, pieces):
    n_pieces = len(pieces)
    rows, width = pieces[0].shape
    block = 256
    return pl.pallas_call(
        mix_kernel,
        grid=(width // block,),
        in_specs=[pl.BlockSpec((width, block), lambda i: (0, i))]
        + [pl.BlockSpec((rows, width), lambda i: (0, 0))] * n_pieces,
        out_specs=pl.BlockSpec((n_pieces, rows, block), lambda i: (0, 0, i)),
        out_shape=jax.ShapeDtypeStruct((n_pieces, rows, width), F32),
        compiler_params=pltpu.CompilerParams(vmem_limit_bytes=VMEM_LIMIT),
        cost_estimate=pl.CostEstimate(
            flops=6 * n_pieces * rows * width * width,
            bytes_accessed=4 * (width * width + 2 * n_pieces * rows * width),
            transcendentals=0,
        ),
        name="mix",
    )(matrix, *pieces)


def spread_kernel(count, holes_ref, *refs):
    loads = refs[:-3]
    pairs = [loads[:1]] + [loads[k : k + 2] for k in range(1, len(loads), 2)]
    out_ref, high_ref, low_ref = refs[-3:]
    segments = pl.num_programs(0)
    segment = pl.program_id(0)
    spans = [(pair, first) for pair in pairs for first in range(0, pair[0].shape[0], count + 8)]

    @pl.when(segment == 0)
    def _():
        for number, (pair, first) in enumerate(spans):
            high, low = halves(sum(load[first : first + count, :] for load in pair))
            high_ref[number * count : (number + 1) * count, :] = high
            low_ref[number * count : (number + 1) * count, :] = low

    wanted = jnp.where(holes_ref[...] >= 0, holes_ref[...] * segments + segment, -1)
    chosen = []
    for pair, first in spans:
        named = sum(load[first + count : first + count + 1, :count] for load in pair).astype(jnp.int32)
        chosen.append(jnp.where(wanted == named, 1.0, 0.0))
    chosen = jnp.concatenate(chosen, axis=1).astype(BF16)
    nn = ((1,), (0,))
    out_ref[...] = dot(chosen, high_ref[...], nn) + dot(chosen, low_ref[...], nn)


def spread(holes, loads, segments, count):
    rows = holes.shape[0]
    height, part = loads[0].shape
    held = (len(loads) + 1) // 2 * (height // (count + 8)) * count
    return pl.pallas_call(
        functools.partial(spread_kernel, count),
        grid=(segments,),
        in_specs=[pl.BlockSpec((rows, 1), lambda i: (0, 0))]
        + [pl.BlockSpec((height, part), lambda i: (0, 0))] * len(loads),
        out_specs=pl.BlockSpec((rows, part), lambda i: (0, i)),
        out_shape=jax.ShapeDtypeStruct((rows, segments * part), F32),
        scratch_shapes=[pltpu.VMEM((held, part), BF16)] * 2,
        compiler_params=pltpu.CompilerParams(vmem_limit_bytes=VMEM_LIMIT),
        cost_estimate=pl.CostEstimate(
            flops=rows * segments * part,
            bytes_accessed=rows * segments * part,
            transcendentals=0,
        ),
        name="spread",
    )(holes, *loads)


def update_kernel(core_ref, driving_ref, denominator_ref, kept_ref, received_ref, *refs):
    out_ref = refs[-1]
    part = kept_ref.shape[1]
    for half in range(2):
        lanes = slice(half * part, (half + 1) * part)
        value = jnp.where(core_ref[0] == half, kept_ref[...], received_ref[...])
        out_ref[:, lanes] = (driving_ref[:, lanes] + value) / denominator_ref[:, lanes]


def update(core, target, driving, denominator, kept, received, offset, part):
    own, width = driving.shape
    size = min(kept.shape[0], own - offset)
    tile = next(rows for rows in (32, 16, 8) if offset % rows == 0 and rows <= size)
    lines = pl.BlockSpec((tile, 2 * part), lambda i, j, core: (offset // tile + i, j))
    half = pl.BlockSpec((tile, part), lambda i, j, core: (i, j))
    return pl.pallas_call(
        update_kernel,
        grid_spec=pltpu.PrefetchScalarGridSpec(
            num_scalar_prefetch=1,
            grid=(pl.cdiv(size, tile), width // (2 * part)),
            in_specs=[lines, lines, half, half] + [pl.BlockSpec(memory_space=pl.ANY)] * len(target),
            out_specs=lines,
        ),
        out_shape=jax.ShapeDtypeStruct((own, width), F32),
        input_output_aliases={5: 0} if target else {},
        compiler_params=pltpu.CompilerParams(vmem_limit_bytes=VMEM_LIMIT),
        cost_estimate=pl.CostEstimate(flops=size * width, bytes_accessed=size * width, transcendentals=0),
        name="update",
    )(core, driving, denominator, kept, received, *target)


def on_device(
    amplitude,
    ladder_coupling,
    crossed_coupling,
    channel_slot,
    channel_of,
    source_row,
    target_row,
    recoupling,
    driving,
    denominator,
):
    groups = lax.axis_size("row")
    columns = lax.axis_size("col")
    depth = columns // 2
    r = lax.axis_index("row")
    c = lax.axis_index("col")
    z, core = c // 2, c % 2
    inner = amplitude.shape[1]
    own = driving.shape[0]
    width = crossed_coupling.shape[1]
    part = width // 2
    count = source_row.shape[1]
    assert depth == groups and amplitude.shape[0] == 2 * own

    across = [[(i, i ^ k) for i in range(groups)] for k in range(1, groups)]
    swap = [(i, i ^ 1) for i in range(columns)]

    def at(array, index):
        return lax.dynamic_index_in_dim(array, index, 0, keepdims=False)

    padded = -(-own // 4) * 4
    sizes = chunk_sizes(padded)
    offsets = [sum(sizes[:k]) for k in range(len(sizes))]
    pairs = jnp.pad(amplitude.reshape(2, own, inner), ((0, 0), (0, padded - own), (0, 0)))
    locals_ = [
        pairs[:, offset : offset + size].reshape(2 * size, inner) for size, offset in zip(sizes, offsets)
    ]

    def spread_first(local, whole):
        return [local] + [lax.ppermute(local, "row", perm) for perm in (across if whole else across[:2])]

    def spread_rest(pieces):
        if len(pieces) == groups:
            return pieces
        cut = pieces[0].shape[0] // 16 * 8
        top = lax.ppermute(pieces[2][:cut], "row", across[0])
        bottom = lax.ppermute(pieces[1][cut:], "row", across[1])
        return [*pieces, top, bottom]

    def tie(*arrays):
        return lax.optimization_barrier(arrays)

    owners = channel_slot[channel_of[0, :, 0]]
    onehot = (owners[:, None] == jnp.arange(groups, dtype=jnp.int32)[None, :]).astype(jnp.int32)
    before = jnp.cumsum(onehot, axis=0) - onehot
    slot = owners * CAP + jnp.sum(before * onehot, axis=1)
    in_slot = slot[None, :] == jnp.arange(groups * CAP, dtype=jnp.int32)[:, None]
    used = jnp.any(in_slot, axis=1)
    source = jnp.sum(jnp.where(in_slot, source_row, 0), axis=1)
    factor = jnp.sum(jnp.where(in_slot, recoupling, 0.0), axis=1)
    per_row = inner // width
    hole, segment = source // per_row, source % per_row
    place = jnp.full_like(hole, -1)
    for size, offset in zip(sizes, offsets):
        inside = hole % own - offset
        spot = 2 * groups * offset + ((hole // (2 * own)) ^ r) * 2 * size + (hole // own % 2) * size + inside
        place = jnp.where((inside >= 0) & (inside < size), spot, place)
    place = jnp.where(used, place, -1)
    names = jnp.pad(target_row[:1].astype(F32), ((0, 7), (0, part - count)))

    last = len(sizes) - 1
    square = groups == 4
    chunks = [spread_rest(spread_first(locals_[0], not square))]
    theirs = jnp.stack([r, 1 - core]).astype(jnp.int32)
    ours = jnp.stack([r, core]).astype(jnp.int32)
    place, segment, factor, names, theirs, ours, *locals_ = tie(
        place[:, None], segment[:, None], factor[:, None], names, theirs, ours, *locals_
    )
    theirs, *chunks[0] = tie(theirs, *chunks[0])

    def gather_chunks():
        held = None
        for kernel in range(last + 1):
            rest = [] if held is None else spread_rest(held)
            first = spread_first(locals_[kernel + 1], not square) if kernel < last else []
            flight = yield None, rest + first
            if rest:
                chunks.append(flight[: len(rest)])
            held = flight[len(rest) :]

    loads = []

    def exchange_segments():
        picked = pick(place, segment, factor, chunks, groups, width)
        arrived = yield picked, [at(picked, r)] + [
            lax.ppermute(at(picked, r ^ k), "row", across[k - 1]) for k in range(1, groups)
        ]
        product = mix(crossed_coupling[0], arrived)
        returned = yield product, [product[0]] + [
            lax.ppermute(product[k], "row", across[k - 1]) for k in range(1, groups)
        ]
        crossed = jnp.concatenate(returned, axis=0)[((slot // CAP) ^ r) * CAP + slot % CAP]
        first = jnp.concatenate([crossed[:, :part], names], axis=0)
        second = jnp.concatenate([crossed[:, part:], names], axis=0)
        to_keep = jnp.where(core == 0, first, second)
        to_send = jnp.where(core == 0, second, first)
        load = jnp.concatenate([to_keep, lax.ppermute(to_send, "col", swap)], axis=0)
        right, left = [load], [load]
        for step in range(depth - 1):
            up = [(i, i + 2) for i in range(columns - 2) if i // 2 >= step]
            down = [(columns - 1 - i, columns - 1 - j) for i, j in up]
            flight = [lax.ppermute(right[-1], "col", up), lax.ppermute(left[-1], "col", down)]
            moved = yield load, flight
            right.append(moved[0])
            left.append(moved[1])
        loads.append(load)
        for k in range(1, depth):
            loads.extend([right[k], left[depth - k]])

    holes = []
    for size, offset in zip(sizes, offsets):
        inside = jnp.tile(jnp.arange(size, dtype=jnp.int32) + offset, 2)
        second = jnp.repeat(jnp.arange(2, dtype=jnp.int32), size)
        holes.append(jnp.where(inside < own, (2 * z + second) * own + inside, -1))
    holes = jnp.concatenate(holes)[:, None]

    lines = [list(range(k, columns, 2)) for k in (0, 1)]
    reduced = {}

    def scatter_line(number, value):
        reduced[number] = lax.psum_scatter(
            value.reshape(depth * 2 * sizes[number], -1),
            "col",
            scatter_dimension=0,
            axis_index_groups=lines,
            tiled=True,
        )

    def walk_line(number, value):
        def own_sum(owner):
            return at(value, jnp.clip(owner, 0, depth - 1))

        right, left = None, None
        for step in range(depth - 1):
            to_right, to_left = own_sum(depth - 1 - step + z), own_sum(z - (depth - 1) + step)
            if step:
                to_right, to_left = to_right + right, to_left + left
            up = [(i, i + 2) for i in range(columns - 2) if i // 2 <= step]
            down = [(columns - 1 - i, columns - 1 - j) for i, j in up]
            right, left = yield None, [lax.ppermute(to_right, "col", up), lax.ppermute(to_left, "col", down)]
        reduced[number] = own_sum(z) + right + left

    gathering, exchanging = gather_chunks(), exchange_segments()
    walks, sent = [], None
    moved = {}

    def begin(stage):
        try:
            return stage.send(moved.pop(stage, None))
        except StopIteration:
            return None, None

    for kernel in range(2 * len(sizes)):
        number, keeping = kernel // 2, kernel % 2
        token, after = (ours, theirs) if keeping else (theirs, ours)
        stages = []
        if kernel < last:
            locals_[kernel + 1], token = tie(locals_[kernel + 1], token)
        if kernel <= last:
            stages.append(gathering)
        else:
            stages.append(exchanging)
        stages += walks
        flights = {}
        for stage in stages:
            ahead, flight = begin(stage)
            if ahead is not None:
                ahead, token = tie(ahead, token)
            if flight is not None:
                flights[stage] = flight
        if keeping:
            received = lax.ppermute(sent, "col", swap)
            value = ladder(token, chunks[number], ladder_coupling, width, received)
        else:
            value = ladder(token, chunks[number], ladder_coupling, width)
        flat = [array for flight in flights.values() for array in flight]
        value, after, *flat = tie(value, after, *flat)
        for stage, flight in flights.items():
            moved[stage], flat = flat[: len(flight)], flat[len(flight) :]
        if kernel == last:
            chunks.append(moved.pop(gathering))
        if not keeping:
            ours, sent = after, value
            continue
        theirs = after
        if number - 1 in reduced:
            value, reduced[number - 1] = tie(value, reduced[number - 1])
        if number < 2:
            scatter_line(number, value)
        else:
            walks.append(walk_line(number, value))
    while len(reduced) < len(sizes) or not loads:
        flights = {stage: begin(stage)[1] for stage in [exchanging] * (not loads) + walks}
        flights = {stage: flight for stage, flight in flights.items() if flight is not None}
        flat = [array for flight in flights.values() for array in flight]
        flat = list(tie(*flat)) if flat else []
        for stage, flight in flights.items():
            moved[stage], flat = flat[: len(flight)], flat[len(flight) :]
    added = spread(holes, loads, ladder_coupling.shape[0] // width, count)

    out = []
    for number, (size, offset) in enumerate(zip(sizes, offsets)):
        line = reduced[number]
        if number == last:
            line, *out = tie(line, *out)
        line = (line + added[2 * offset : 2 * (offset + size)]).reshape(2, size, -1)
        received = lax.ppermute(at(line, 1 - core), "col", swap)
        out = [update(core[None], out, driving, denominator, at(line, core), received, offset, part)]
    return out[0]


def solution(mesh):
    in_specs = (
        P("row", "col"),
        P("row", "col"),
        P("row", None, None),
        P(),
        P("col", "row", None),
        P("col", "row"),
        P("col", "row"),
        P("col", "row"),
        P("col", "row"),
        P("col", "row"),
    )
    out_specs = P("col", "row")
    return jax.shard_map(
        on_device, mesh=mesh, in_specs=in_specs, out_specs=out_specs, check_vma=False
    )
```

time: 508 us -> 316 us (0.62)
  blocking collectives: 181 us -> 0 us
  Pallas kernels: 0 us -> 153 us
  matrix products: 143 us -> 0 us
  starting transfers between devices: 8.86 us -> 56.9 us
  waiting for transfers between devices: 96.2 us -> 51.8 us
  local copies, waits for them, and re-layouts: 37 us -> 21.6 us
  other arithmetic: 24.4 us -> 18 us
    unnamed x1 -> x0, blocking collectives: 168 us -> none
    pallas_call x0 -> x12, Pallas kernels: none -> 153 us  [the longest x6 120 us: ladder(): pl.pallas_call(functools.partial(ladder_kernel, len(pieces)), grid_spec=p...]
    dot_general x2 -> x0, matrix products: 143 us -> none  [the longest x1 136 us: on_device(): lax.dot_general(gathered, ladder_coupling, (((1,), (1,)), ((), ())), prec...]
    all_gather x1 -> x0, waiting for transfers between devices: 80.1 us -> none  [on_device(): gathered = lax.all_gather(amplitude, 'row', axis=0, tiled=True)]
    ppermute x0 -> x37, starting transfers between devices: none -> 56.6 us  [the longest x3 12.8 us: exchange_segments(): lax.ppermute(right[-1], 'col', up)]
    ppermute x0 -> x37, waiting for transfers between devices: none -> 49.1 us  [the longest x3 13.6 us: exchange_segments(): lax.ppermute(right[-1], 'col', up)]
    reshape x2 -> x3, local copies, waits for them, and re-layouts: 27.6 us -> 3.08 us  [the longest x1 1.77 us: on_device(): amplitude.reshape(2, own, inner)]
    all_to_all x1 -> x0, blocking collectives: 12.8 us -> none  [on_device(): lax.all_to_all(buffer, 'row', split_axis=0, concat_axis=0, tiled=True)]
  transfers between devices with their start and end apart: 3 -> 39, of which waited for: 3 -> 14; matrix products, arithmetic and copies ran while one was open for 2% -> 8% of each run, Pallas kernels for 0% -> 47%
where the time goes in v1:
time: 316 us; the launch traced here: 315 us
  Pallas kernels  153 us (48%)
  starting transfers between devices  56.9 us (18%)
  waiting for transfers between devices  51.8 us (16%)
  local copies, waits for them, and re-layouts  21.6 us (7%)
  other arithmetic  18 us (6%)
  between operations  14 us (4%)
    pallas_call x6, Pallas kernels, ladder(): pl.pallas_call(functools.partial(ladder_kernel, len(pieces)), grid_spec=p...  120 us
    ppermute x3, waiting for transfers between devices, exchange_segments(): lax.ppermute(right[-1], 'col', up)  13.6 us
    ppermute x3, starting transfers between devices, exchange_segments(): lax.ppermute(right[-1], 'col', up)  12.8 us
    pallas_call x3, Pallas kernels, update(): pl.pallas_call(update_kernel, grid_spec=pltpu.PrefetchScalarGridSpec(num_...  12.6 us
    ppermute x3, waiting for transfers between devices, walk_line(): lax.ppermute(to_left, 'col', down)  9.78 us
    ppermute x3, starting transfers between devices, walk_line(): lax.ppermute(to_right, 'col', up)  7.42 us
    pallas_call x1, Pallas kernels, spread(): pl.pallas_call(functools.partial(spread_kernel, count), grid=(segments,),...  7.4 us
    squeeze x5, local copies, waits for them, and re-layouts, at(): return lax.dynamic_index_in_dim(array, index, 0, keepdims=False)  7.39 us
  transfers between devices with their start and end apart: 39, of which 14 were waited for; matrix products, arithmetic and copies ran while one was open for 8% of the time, Pallas kernels for 47%

profile of v1, /device:TPU:21, one launch (start us, length us, event | category | flops | bytes accessed | tf_op | source)
XLA Modules:
  0.0 315.0 jit_solution(14996882674710706782)
XLA Ops:
  6.5 1.8 reshape.421
  8.8 1.2 collective-permute-start
  11.6 2.5 fusion.12
  14.6 2.6 fusion.13
  17.4 1.2 reshape.424.refs_10_.refs_0_
  18.9 5.3 %collective-permute-done.1.refs_2_ = f32[64,2560]{1,0:T(8,128)} collective-permute-done((f32[64,2560]{1,0:T(8,128)S(1)}, f32[64,2560]{1,0:T(8,128)}, u32[]{:S(2)}, u32[]{:S(2)}) %collective-permute-start.1) | collective-permute-done | bytes 655392 | tf_op jit(solution)/shard_map/ppermute | solution.py:267
  25.3 1.3 collective-permute-start.2
  26.5 1.0 slice.83
  29.4 3.5 %collective-permute-done.2.refs_3_ = f32[32,2560]{1,0:T(8,128)S(1)} collective-permute-done((f32[32,2560]{1,0:T(8,128)S(1)}, f32[32,2560]{1,0:T(8,128)S(1)}, u32[]{:S(2)}, u32[]{:S(2)}) %collective-permute-start.2) | collective-permute-done | bytes 327712 | tf_op jit(solution)/shard_map/ppermute | solution.py:273
  33.0 2.0 collective-permute-done.3.refs_4_
  35.7 17.4 %ladder.6 = f32[4,64,2560]{2,1,0:T(8,128)} custom-call(s32[2]{0:T(128)} %get-tuple-element.123.where_ref, f32[64,2560]{1,0:T(8,128)} %bitcast.101, f32[64,2560]{1,0:T(8,128)} %collective-permute-done.refs_1_, f32[64,2560]{1,0:T(8,128)} %collective-permute-done.1.refs_2_, f32[32,2560]{1,0:T(8,128)} %copy-done.9, f32[32,2560]{1,0:T(8,128)} %copy-done.10, ...), custom_call_target="tpu_custom_call" | custom-call | flops 1677721600 | bytes 1638400 | tf_op jit(solution)/shard_map/ladder/pallas_call | solution.py:62
  53.2 3.1 collective-permute-start.6
  56.3 1.3 collective-permute-start.10
  57.5 1.2 collective-permute-start.9
  59.4 1.7 collective-permute-done.6.refs_6_
  61.0 1.5 copy-done.14
  62.5 17.8 %ladder.7 = f32[4,64,2560]{2,1,0:T(8,128)} custom-call(s32[2]{0:T(128)} %get-tuple-element.130.where_ref, f32[64,2560]{1,0:T(8,128)} %bitcast.102, f32[64,2560]{1,0:T(8,128)} %collective-permute-done.refs_1_, f32[64,2560]{1,0:T(8,128)} %collective-permute-done.1.refs_2_, f32[32,2560]{1,0:T(8,128)} %copy-done.9, f32[32,2560]{1,0:T(8,128)} %copy-done.10, ...), custom_call_target="tpu_custom_call" | custom-call | flops 1677721600 | bytes 1638400 | tf_op jit(solution)/shard_map/ladder/pallas_call | solution.py:62
  80.3 2.0 collective-permute-done.7.refs_3_.refs_8_
  83.0 1.3 collective-permute-start.11
  84.3 17.6 %ladder.8 = f32[4,64,2560]{2,1,0:T(8,128)} custom-call(s32[2]{0:T(128)} %get-tuple-element.123.where_ref, f32[64,2560]{1,0:T(8,128)} %bitcast.96, f32[64,2560]{1,0:T(8,128)} %copy-done.7, f32[64,2560]{1,0:T(8,128)} %copy-done.6, f32[32,2560]{1,0:T(8,128)} %copy-done.11, f32[32,2560]{1,0:T(8,128)} %copy-done.12, f32[5120,2560]{1,0:T(8,128)} %refs_5_.11), custom_call_target="tpu_custom_call" | custom-call | flops 1677721600 | bytes 1638400 | tf_op jit(solution)/shard_map/ladder/pallas_call | solution.py:62
  101.9 1.6 collective-permute-start.13
  104.3 6.4 %pick.1 = f32[4,40,1280]{2,1,0:T(8,128)} custom-call(s32[160,1]{1,0:T(8,128)} %get-tuple-element.79.place_ref, s32[160,1]{1,0:T(8,128)} %get-tuple-element.80.segment_ref, f32[160,1]{1,0:T(8,128)} %copy.25.factor_ref, f32[64,2560]{1,0:T(8,128)} %bitcast.103, f32[64,2560]{1,0:T(8,128)} %collective-permute-done.refs_1_, ...), custom_call_target="tpu_custom_call" | custom-call | flops 204800 | bytes 204800 | tf_op jit(solution)/shard_map/pick/pallas_call | solution.py:109
  110.7 2.0 dynamic-slice_bitcast_fusion.8
  112.7 1.2 collective-permute-start.16
  114.1 1.2 collective-permute-start.14
  115.3 17.8 %ladder.9 = f32[4,64,2560]{2,1,0:T(8,128)} custom-call(s32[2]{0:T(128)} %get-tuple-element.130.where_ref, f32[64,2560]{1,0:T(8,128)} %bitcast.98, f32[64,2560]{1,0:T(8,128)} %copy-done.7, f32[64,2560]{1,0:T(8,128)} %copy-done.6, f32[32,2560]{1,0:T(8,128)} %copy-done.11, f32[32,2560]{1,0:T(8,128)} %copy-done.12, f32[5120,2560]{1,0:T(8,128)} %refs_5_.11, ...), custom_call_target="tpu_custom_call" | custom-call | flops 1677721600 | bytes 1638400 | tf_op jit(solution)/shard_map/ladder/pallas_call | solution.py:62
  133.2 2.7 reduce-scatter.3.cloned.1.call-done
  136.0 6.5 %mix.1 = f32[4,40,1280]{2,1,0:T(8,128)} custom-call(f32[1280,1280]{1,0:T(8,128)} %bitcast.106, f32[40,1280]{1,0:T(8,128)} %get-tuple-element.118.refs_0_, f32[40,1280]{1,0:T(8,128)} %copy-done.21, f32[40,1280]{1,0:T(8,128)} %copy-done.20, f32[40,1280]{1,0:T(8,128)} %copy-done.19), custom_call_target="tpu_custom_call" | custom-call | flops 1572864000 | bytes 8192000 | tf_op jit(solution)/shard_map/mix/pallas_call | solution.py:132
  142.5 1.3 slice_bitcast_fusion
  143.8 1.2 collective-permute-start.19
  145.0 1.2 collective-permute-start.18
  146.5 24.5 %ladder.10 = f32[4,72,2560]{2,1,0:T(8,128)} custom-call(s32[2]{0:T(128)} %get-tuple-element.123.where_ref, f32[72,2560]{1,0:T(8,128)} %copy-done.1, f32[72,2560]{1,0:T(8,128)} %copy-done.4, f32[72,2560]{1,0:T(8,128)} %copy-done.5, f32[32,2560]{1,0:T(8,128)} %copy-done.13, f32[40,2560]{1,0:T(8,128)} %copy-done.8, f32[5120,2560]{1,0:T(8,128)} %refs_5_.11), custom_call_target="tpu_custom_call" | custom-call | flops 1887436800 | bytes 1638400 | tf_op jit(solution)/shard_map/ladder/pallas_call | solution.py:62
  171.1 1.6 collective-permute-start.21
  173.8 4.3 %collective-permute-done.20 = f32[136,640]{1,0:T(8,128)S(1)} collective-permute-done((f32[136,640]{1,0:T(8,128)S(1)}, f32[136,640]{1,0:T(8,128)S(1)}, u32[]{:S(2)}, u32[]{:S(2)}) %collective-permute-start.20) | collective-permute-done | bytes 348192 | tf_op jit(solution)/shard_map/ppermute | solution.py:334
  179.1 1.9 collective-permute-start.23
  181.0 4.2 %collective-permute-start.22 = (f32[272,640]{1,0:T(8,128)}, f32[272,640]{1,0:T(8,128)}, u32[]{:S(2)}, u32[]{:S(2)}) collective-permute-start(f32[272,640]{1,0:T(8,128)} %pad_maximum_fusion.1.refs_0_), channel_id=1, source_target_pairs={{0,2},{1,3},{2,4},{3,5},{4,6},{5,7},{8,10},{9,11},{10,12},{11,13},... | collective-permute-start | bytes 2088968 | tf_op jit(solution)/shard_map/ppermute | solution.py:339
  185.2 24.7 %ladder.11 = f32[4,72,2560]{2,1,0:T(8,128)} custom-call(s32[2]{0:T(128)} %get-tuple-element.130.where_ref, f32[72,2560]{1,0:T(8,128)} %copy-done.1, f32[72,2560]{1,0:T(8,128)} %copy-done.4, f32[72,2560]{1,0:T(8,128)} %copy-done.5, f32[32,2560]{1,0:T(8,128)} %copy-done.13, f32[40,2560]{1,0:T(8,128)} %copy-done.8, f32[5120,2560]{1,0:T(8,128)} %refs_5_.11, ...), custom_call_target="tpu_custom_call" | custom-call | flops 1887436800 | bytes 1638400 | tf_op jit(solution)/shard_map/ladder/pallas_call | solution.py:62
  209.9 2.8 dynamic-slice_bitcast_fusion
  212.7 1.3 collective-permute-start.27
  214.0 1.5 collective-permute-start.26
  215.5 4.8 %collective-permute-start.24 = (f32[272,640]{1,0:T(8,128)}, f32[272,640]{1,0:T(8,128)}, u32[]{:S(2)}, u32[]{:S(2)}) collective-permute-start(f32[272,640]{1,0:T(8,128)} %collective-permute-done.22.refs_1_), channel_id=1, source_target_pairs={{2,4},{3,5},{4,6},{5,7},{10,12},{11,13},{12,14},{13,15},{18,20},{1... | collective-permute-start | bytes 2088968 | tf_op jit(solution)/shard_map/ppermute | solution.py:339
  220.4 2.2 collective-permute-start.25
  222.5 11.8 %collective-permute-done.24.refs_3_ = f32[272,640]{1,0:T(8,128)} collective-permute-done((f32[272,640]{1,0:T(8,128)}, f32[272,640]{1,0:T(8,128)}, u32[]{:S(2)}, u32[]{:S(2)}) %collective-permute-start.24) | collective-permute-done | bytes 696352 | tf_op jit(solution)/shard_map/ppermute | solution.py:339
  234.4 1.3 collective-permute-done.25.refs_4_
  235.7 3.7 %collective-permute-start.28 = (f32[272,640]{1,0:T(8,128)}, f32[272,640]{1,0:T(8,128)}, u32[]{:S(2)}, u32[]{:S(2)}) collective-permute-start(f32[272,640]{1,0:T(8,128)} %collective-permute-done.24.refs_3_), channel_id=1, source_target_pairs={{4,6},{5,7},{12,14},{13,15},{20,22},{21,23},{28,30},{29,31}} | collective-permute-start | bytes 2088968 | tf_op jit(solution)/shard_map/ppermute | solution.py:339
  239.4 1.5 collective-permute-start.29
  240.9 2.6 bitcast_add_fusion.1
  243.6 3.5 %collective-permute-start.31 = (f32[72,2560]{1,0:T(8,128)}, f32[72,2560]{1,0:T(8,128)}, u32[]{:S(2)}, u32[]{:S(2)}) collective-permute-start(f32[72,2560]{1,0:T(8,128)} %get-tuple-element.157), channel_id=1, source_target_pairs={{7,5},{6,4},{5,3},{4,2},{15,13},{14,12},{13,11},{12,10},{23,21},{2... | collective-permute-start | bytes 2211848 | tf_op jit(solution)/shard_map/ppermute | solution.py:377
  247.0 1.6 collective-permute-start.30
  249.7 1.8 collective-permute-done.28.refs_5_
  251.6 9.8 %collective-permute-done.31 = f32[72,2560]{1,0:T(8,128)} collective-permute-done((f32[72,2560]{1,0:T(8,128)}, f32[72,2560]{1,0:T(8,128)}, u32[]{:S(2)}, u32[]{:S(2)}) %collective-permute-start.31) | collective-permute-done | bytes 737312 | tf_op jit(solution)/shard_map/ppermute | solution.py:377
  261.3 3.5 %collective-permute-done.30 = f32[72,2560]{1,0:T(8,128)} collective-permute-done((f32[72,2560]{1,0:T(8,128)}, f32[72,2560]{1,0:T(8,128)}, u32[]{:S(2)}, u32[]{:S(2)}) %collective-permute-start.30) | collective-permute-done | bytes 737312 | tf_op jit(solution)/shard_map/ppermute | solution.py:377
  264.8 2.6 bitcast_add_fusion
  267.4 1.9 collective-permute-start.33
  269.4 4.3 %collective-permute-start.32 = (f32[72,2560]{1,0:T(8,128)}, f32[72,2560]{1,0:T(8,128)}, u32[]{:S(2)}, u32[]{:S(2)}) collective-permute-start(f32[72,2560]{1,0:T(8,128)} %get-tuple-element.156), channel_id=1, source_target_pairs={{0,2},{1,3},{2,4},{3,5},{4,6},{5,7},{8,10},{9,11},{10,12},{11,13},... | collective-permute-start | bytes 2211848 | tf_op jit(solution)/shard_map/ppermute | solution.py:377
  273.7 7.4 %spread.1 = f32[200,2560]{1,0:T(8,128)} custom-call(s32[200,1]{1,0:T(8,128)} %copy.26.holes_ref, f32[272,640]{1,0:T(8,128)} %pad_maximum_fusion.1.refs_0_, f32[272,640]{1,0:T(8,128)} %collective-permute-done.22.refs_1_, f32[272,640]{1,0:T(8,128)} %collective-permute-done.29.refs_2_, f32[272,640]{1,0:T(8,128)} %collective-permute-done.24.refs_3_, ...), custom_call_target="tpu_custom_call" | custom-call | flops 512000 | bytes 512000 | tf_op jit(solution)/shard_map/spread/pallas_call | solution.py:178
  281.1 1.4 slice_add_fusion.1
  283.5 3.9 %collective-permute-start.35 = (f32[32,2560]{1,0:T(8,128)}, f32[32,2560]{1,0:T(8,128)S(1)}, u32[]{:S(2)}, u32[]{:S(2)}) collective-permute-start(f32[32,2560]{1,0:T(8,128)} %get-tuple-element.177), channel_id=1, source_target_pairs={{0,1},{1,0},{2,3},{3,2},{4,5},{5,4},{6,7},{7,6},{8,9},{9,8},{10,11... | collective-permute-start | bytes 983048 | tf_op jit(solution)/shard_map/ppermute | solution.py:444
  289.5 3.6 %update.3.refs_0_ = f32[100,5120]{1,0:T(8,128)} custom-call(s32[1]{0:T(128)} %bitcast.core_ref, f32[100,5120]{1,0:T(8,128)} %driving_ref.5, f32[100,5120]{1,0:T(8,128)} %denominator_ref.5, f32[32,2560]{1,0:T(8,128)} %get-tuple-element.178.kept_ref, f32[32,2560]{1,0:T(8,128)} %copy-done.18), custom_call_target="tpu_custom_call" | custom-call | flops 163840 | bytes 163840 | tf_op jit(solution)/shard_map/update/pallas_call | solution.py:211
  293.1 3.6 %update.4.refs_0_ = f32[100,5120]{1,0:T(8,128)} custom-call(s32[1]{0:T(128)} %bitcast.core_ref, f32[100,5120]{1,0:T(8,128)} %driving_ref.5, f32[100,5120]{1,0:T(8,128)} %denominator_ref.5, f32[32,2560]{1,0:T(8,128)} %get-tuple-element.180.kept_ref, f32[32,2560]{1,0:T(8,128)} %collective-permute-done.34.received_ref, ...), custom_call_target="tpu_custom_call", output_to_operand_aliasing={{}: (5, {})} | custom-call | flops 163840 | bytes 163840 | tf_op jit(solution)/shard_map/update/pallas_call | solution.py:211
  296.7 1.5 fusion
  298.1 1.2 slice_add_fusion
  300.6 1.4 collective-permute-done.36.received_ref
  302.7 5.4 %update.5 = f32[100,5120]{1,0:T(8,128)} custom-call(s32[1]{0:T(128)} %bitcast.core_ref, f32[100,5120]{1,0:T(8,128)} %driving_ref.5, f32[100,5120]{1,0:T(8,128)} %denominator_ref.5, f32[36,2560]{1,0:T(8,128)} %get-tuple-element.166.kept_ref, f32[36,2560]{1,0:T(8,128)} %copy-done.17, f32[100,5120]{1,0:T(8,128)} %update.4.refs_0_), custom_call_target="tpu_custom_call", output_to_operand_aliasing={{}: (5, {})} | custom-call | flops 184320 | bytes 184320 | tf_op jit(solution)/shard_map/update/pallas_call | solution.py:211
  (136 shorter events, 17.6 us)
Async XLA Ops:
  6.5 129.4 %reduce-scatter.3.cloned.1.call-start = ((), (), s32[]{:S(2)}) async-start(), calls=%async_computation.2 | async-start | bytes 3276800 | tf_op jit(solution)/shard_map/reduce_scatter | solution.py:358
  8.3 2.6 copy-start.26
  8.3 2.6 copy-start.22
  8.3 3.3 %copy-start.23 = (s32[1,128,1]{1,2,0:T(1,128)S(1)}, s32[1,128,1]{1,2,0:T(1,128)}, u32[]{:S(2)}) copy-start(s32[1,128,1]{1,2,0:T(1,128)} %param.14) | copy-start | bytes 1540
  8.4 8.8 %copy-start.24 = (s32[1,128]{1,0:T(1,128)S(1)}, s32[1,128]{1,0:T(1,128)}, u32[]{:S(2)}) copy-start(s32[1,128]{1,0:T(1,128)} %param.15) | copy-start | bytes 1540
  8.4 10.5 %copy-start.25 = (f32[1,128]{1,0:T(1,128)S(1)}, f32[1,128]{1,0:T(1,128)}, u32[]{:S(2)}) copy-start(f32[1,128]{1,0:T(1,128)} %param.17) | copy-start | bytes 1540
  8.5 27.0 %copy-start.3 = (f32[2,32,2560]{2,1,0:T(8,128)}, f32[2,32,2560]{2,1,0:T(8,128)S(1)}, u32[]{:S(2)}) copy-start(f32[2,32,2560]{2,1,0:T(8,128)S(1)} %get-tuple-element.162) | copy-start | bytes 1966084
  8.5 44.6 %copy-start.2 = (f32[2,32,2560]{2,1,0:T(8,128)}, f32[2,32,2560]{2,1,0:T(8,128)S(1)}, u32[]{:S(2)}) copy-start(f32[2,32,2560]{2,1,0:T(8,128)S(1)} %get-tuple-element.161) | copy-start | bytes 1966084
  8.5 15.8 %collective-permute-start.1 = (f32[64,2560]{1,0:T(8,128)S(1)}, f32[64,2560]{1,0:T(8,128)}, u32[]{:S(2)}, u32[]{:S(2)}) collective-permute-start(f32[64,2560]{1,0:T(8,128)S(1)} %bitcast.99), channel_id=1, source_target_pairs={{0,16},{8,24},{16,0},{24,8},{1,17},{9,25},{17,1},{25,9},{2,18},{10... | collective-permute-start | bytes 1966088 | tf_op jit(solution)/shard_map/ppermute | solution.py:267
  8.8 17.8 %collective-permute-start = (f32[64,2560]{1,0:T(8,128)S(1)}, f32[64,2560]{1,0:T(8,128)}, u32[]{:S(2)}, u32[]{:S(2)}) collective-permute-start(f32[64,2560]{1,0:T(8,128)S(1)} %bitcast.100), channel_id=1, source_target_pairs={{0,8},{8,0},{16,24},{24,16},{1,9},{9,1},{17,25},{25,17},{2,10},{10... | collective-permute-start | bytes 1966088 | tf_op jit(solution)/shard_map/ppermute | solution.py:267
  18.7 38.9 %copy-start.1 = (f32[72,2560]{1,0:T(8,128)}, f32[72,2560]{1,0:T(8,128)S(1)}, u32[]{:S(2)}) copy-start(f32[72,2560]{1,0:T(8,128)S(1)} %reshape.424.refs_10_.refs_0_) | copy-start | bytes 2211844
  25.3 7.7 %collective-permute-start.2 = (f32[32,2560]{1,0:T(8,128)S(1)}, f32[32,2560]{1,0:T(8,128)S(1)}, u32[]{:S(2)}, u32[]{:S(2)}) collective-permute-start(f32[32,2560]{1,0:T(8,128)S(1)} %slice.82), channel_id=1, source_target_pairs={{0,8},{8,0},{16,24},{24,16},{1,9},{9,1},{17,25},{25,17},{2,10},{10... | collective-permute-start | bytes 983048 | tf_op jit(solution)/shard_map/ppermute | solution.py:273
  27.5 7.4 %collective-permute-start.3 = (f32[32,2560]{1,0:T(8,128)S(1)}, f32[32,2560]{1,0:T(8,128)S(1)}, u32[]{:S(2)}, u32[]{:S(2)}) collective-permute-start(f32[32,2560]{1,0:T(8,128)S(1)} %slice.83), channel_id=1, source_target_pairs={{0,16},{8,24},{16,0},{24,8},{1,17},{9,25},{17,1},{25,9},{2,18},{10... | collective-permute-start | bytes 983048 | tf_op jit(solution)/shard_map/ppermute | solution.py:274
  33.0 2.5 copy-start.9
  35.0 18.1 %collective-permute-start.5 = (f32[64,2560]{1,0:T(8,128)S(1)}, f32[64,2560]{1,0:T(8,128)S(1)}, u32[]{:S(2)}, u32[]{:S(2)}) collective-permute-start(f32[64,2560]{1,0:T(8,128)S(1)} %bitcast.94), channel_id=1, source_target_pairs={{0,16},{8,24},{16,0},{24,8},{1,17},{9,25},{17,1},{25,9},{2,18},{10... | collective-permute-start | bytes 1966088 | tf_op jit(solution)/shard_map/ppermute | solution.py:267
  35.2 17.9 %collective-permute-start.4 = (f32[64,2560]{1,0:T(8,128)S(1)}, f32[64,2560]{1,0:T(8,128)S(1)}, u32[]{:S(2)}, u32[]{:S(2)}) collective-permute-start(f32[64,2560]{1,0:T(8,128)S(1)} %bitcast.95), channel_id=1, source_target_pairs={{0,8},{8,0},{16,24},{24,16},{1,9},{9,1},{17,25},{25,17},{2,10},{10... | collective-permute-start | bytes 1966088 | tf_op jit(solution)/shard_map/ppermute | solution.py:267
  53.1 27.2 %copy-start.6 = (f32[64,2560]{1,0:T(8,128)}, f32[64,2560]{1,0:T(8,128)S(1)}, u32[]{:S(2)}) copy-start(f32[64,2560]{1,0:T(8,128)S(1)} %collective-permute-done.5.refs_2_.refs_7_) | copy-start | bytes 1966084
  53.2 27.1 %copy-start.7 = (f32[64,2560]{1,0:T(8,128)}, f32[64,2560]{1,0:T(8,128)S(1)}, u32[]{:S(2)}) copy-start(f32[64,2560]{1,0:T(8,128)S(1)} %collective-permute-done.4.refs_1_.refs_6_) | copy-start | bytes 1966084
  53.2 7.9 %collective-permute-start.6 = (f32[4,64,2560]{2,1,0:T(8,128)}, f32[4,64,2560]{2,1,0:T(8,128)S(1)}, u32[]{:S(2)}, u32[]{:S(2)}) collective-permute-start(f32[4,64,2560]{2,1,0:T(8,128)} %ladder.6), channel_id=1, source_target_pairs={{0,1},{1,0},{2,3},{3,2},{4,5},{5,4},{6,7},{7,6},{8,9},{9,8},{10,11... | collective-permute-start | bytes 7864328 | tf_op jit(solution)/shard_map/ppermute | solution.py:409
  56.3 26.0 %collective-permute-start.10 = (f32[72,2560]{1,0:T(8,128)S(1)}, f32[72,2560]{1,0:T(8,128)S(1)}, u32[]{:S(2)}, u32[]{:S(2)}) collective-permute-start(f32[72,2560]{1,0:T(8,128)S(1)} %reshape.424.refs_10_.refs_0_), channel_id=1, source_target_pairs={{0,16},{8,24},{16,0},{24,8},{1,17},{9,25},{17,1},{25,9},{2,18},{10... | collective-permute-start | bytes 2211848 | tf_op jit(solution)/shard_map/ppermute | solution.py:267
  57.5 24.8 %collective-permute-start.9 = (f32[72,2560]{1,0:T(8,128)S(1)}, f32[72,2560]{1,0:T(8,128)S(1)}, u32[]{:S(2)}, u32[]{:S(2)}) collective-permute-start(f32[72,2560]{1,0:T(8,128)S(1)} %reshape.424.refs_10_.refs_0_), channel_id=1, source_target_pairs={{0,8},{8,0},{16,24},{24,16},{1,9},{9,1},{17,25},{25,17},{2,10},{10... | collective-permute-start | bytes 2211848 | tf_op jit(solution)/shard_map/ppermute | solution.py:267
  58.8 23.5 %collective-permute-start.7 = (f32[32,2560]{1,0:T(8,128)S(1)}, f32[32,2560]{1,0:T(8,128)S(1)}, u32[]{:S(2)}, u32[]{:S(2)}) collective-permute-start(f32[32,2560]{1,0:T(8,128)S(1)} %slice.59), channel_id=1, source_target_pairs={{0,8},{8,0},{16,24},{24,16},{1,9},{9,1},{17,25},{25,17},{2,10},{10... | collective-permute-start | bytes 983048 | tf_op jit(solution)/shard_map/ppermute | solution.py:273
  59.1 23.2 %collective-permute-start.8 = (f32[32,2560]{1,0:T(8,128)S(1)}, f32[32,2560]{1,0:T(8,128)S(1)}, u32[]{:S(2)}, u32[]{:S(2)}) collective-permute-start(f32[32,2560]{1,0:T(8,128)S(1)} %slice.60), channel_id=1, source_target_pairs={{0,16},{8,24},{16,0},{24,8},{1,17},{9,25},{17,1},{25,9},{2,18},{10... | collective-permute-start | bytes 983048 | tf_op jit(solution)/shard_map/ppermute | solution.py:274
  61.0 1.5 copy-start.14
  82.3 2.0 copy-start.11
  82.3 2.0 copy-start.12
  82.3 19.6 %copy-start.5 = (f32[72,2560]{1,0:T(8,128)}, f32[72,2560]{1,0:T(8,128)S(1)}, u32[]{:S(2)}) copy-start(f32[72,2560]{1,0:T(8,128)S(1)} %collective-permute-done.10.refs_12_.refs_2_) | copy-start | bytes 2211844
  82.3 19.6 %copy-start.4 = (f32[72,2560]{1,0:T(8,128)}, f32[72,2560]{1,0:T(8,128)S(1)}, u32[]{:S(2)}) copy-start(f32[72,2560]{1,0:T(8,128)S(1)} %collective-permute-done.9.refs_11_.refs_1_) | copy-start | bytes 2211844
  82.4 127.6 %reduce-scatter.5.cloned.1.call-start = ((), (), s32[]{:S(2)}) async-start(), calls=%async_computation.3 | async-start | bytes 3276800 | tf_op jit(solution)/shard_map/reduce_scatter | solution.py:358
  82.6 19.3 %collective-permute-start.12 = (f32[40,2560]{1,0:T(8,128)S(1)}, f32[40,2560]{1,0:T(8,128)S(1)}, u32[]{:S(2)}, u32[]{:S(2)}) collective-permute-start(f32[40,2560]{1,0:T(8,128)S(1)} %slice.62), channel_id=1, source_target_pairs={{0,16},{8,24},{16,0},{24,8},{1,17},{9,25},{17,1},{25,9},{2,18},{10... | collective-permute-start | bytes 1228808 | tf_op jit(solution)/shard_map/ppermute | solution.py:274
  83.0 18.9 %collective-permute-start.11 = (f32[32,2560]{1,0:T(8,128)S(1)}, f32[32,2560]{1,0:T(8,128)S(1)}, u32[]{:S(2)}, u32[]{:S(2)}) collective-permute-start(f32[32,2560]{1,0:T(8,128)S(1)} %slice.61), channel_id=1, source_target_pairs={{0,8},{8,0},{16,24},{24,16},{1,9},{9,1},{17,25},{25,17},{2,10},{10... | collective-permute-start | bytes 983048 | tf_op jit(solution)/shard_map/ppermute | solution.py:273
  101.9 2.4 copy-start.13
  101.9 2.4 copy-start.8
  101.9 13.4 %collective-permute-start.13 = (f32[4,64,2560]{2,1,0:T(8,128)}, f32[4,64,2560]{2,1,0:T(8,128)}, u32[]{:S(2)}, u32[]{:S(2)}) collective-permute-start(f32[4,64,2560]{2,1,0:T(8,128)} %ladder.8), channel_id=1, source_target_pairs={{0,1},{1,0},{2,3},{3,2},{4,5},{5,4},{6,7},{7,6},{8,9},{9,8},{10,11... | collective-permute-start | bytes 7864328 | tf_op jit(solution)/shard_map/ppermute | solution.py:409
  112.7 20.5 %collective-permute-start.16 = (f32[40,1280]{1,0:T(8,128)S(1)}, f32[40,1280]{1,0:T(8,128)S(1)}, u32[]{:S(2)}, u32[]{:S(2)}) collective-permute-start(f32[40,1280]{1,0:T(8,128)S(1)} %get-tuple-element.171), channel_id=1, source_target_pairs={{0,24},{8,16},{16,8},{24,0},{1,25},{9,17},{17,9},{25,1},{2,26},{10... | collective-permute-start | bytes 614408 | tf_op jit(solution)/shard_map/ppermute | solution.py:323
  113.9 19.3 %collective-permute-start.15 = (f32[40,1280]{1,0:T(8,128)S(1)}, f32[40,1280]{1,0:T(8,128)S(1)}, u32[]{:S(2)}, u32[]{:S(2)}) collective-permute-start(f32[40,1280]{1,0:T(8,128)S(1)} %get-tuple-element.172), channel_id=1, source_target_pairs={{0,16},{8,24},{16,0},{24,8},{1,17},{9,25},{17,1},{25,9},{2,18},{10... | collective-permute-start | bytes 614408 | tf_op jit(solution)/shard_map/ppermute | solution.py:323
  114.1 19.1 %collective-permute-start.14 = (f32[40,1280]{1,0:T(8,128)S(1)}, f32[40,1280]{1,0:T(8,128)S(1)}, u32[]{:S(2)}, u32[]{:S(2)}) collective-permute-start(f32[40,1280]{1,0:T(8,128)S(1)} %get-tuple-element.173), channel_id=1, source_target_pairs={{0,8},{8,0},{16,24},{24,16},{1,9},{9,1},{17,25},{25,17},{2,10},{10... | collective-permute-start | bytes 614408 | tf_op jit(solution)/shard_map/ppermute | solution.py:323
  133.2 2.8 copy-start.19
  133.2 2.8 copy-start.20
  133.2 2.8 copy-start.21
  143.8 27.3 %collective-permute-start.19 = (f32[40,1280]{1,0:T(8,128)S(1)}, f32[40,1280]{1,0:T(8,128)S(1)}, u32[]{:S(2)}, u32[]{:S(2)}) collective-permute-start(f32[40,1280]{1,0:T(8,128)S(1)} %get-tuple-element.167), channel_id=1, source_target_pairs={{0,24},{8,16},{16,8},{24,0},{1,25},{9,17},{17,9},{25,1},{2,26},{10... | collective-permute-start | bytes 614408 | tf_op jit(solution)/shard_map/ppermute | solution.py:327
  145.0 26.1 %collective-permute-start.18 = (f32[40,1280]{1,0:T(8,128)S(1)}, f32[40,1280]{1,0:T(8,128)S(1)}, u32[]{:S(2)}, u32[]{:S(2)}) collective-permute-start(f32[40,1280]{1,0:T(8,128)S(1)} %get-tuple-element.168), channel_id=1, source_target_pairs={{0,16},{8,24},{16,0},{24,8},{1,17},{9,25},{17,1},{25,9},{2,18},{10... | collective-permute-start | bytes 614408 | tf_op jit(solution)/shard_map/ppermute | solution.py:327
  146.2 24.8 %collective-permute-start.17 = (f32[40,1280]{1,0:T(8,128)S(1)}, f32[40,1280]{1,0:T(8,128)S(1)}, u32[]{:S(2)}, u32[]{:S(2)}) collective-permute-start(f32[40,1280]{1,0:T(8,128)S(1)} %get-tuple-element.169), channel_id=1, source_target_pairs={{0,8},{8,0},{16,24},{24,16},{1,9},{9,1},{17,25},{25,17},{2,10},{10... | collective-permute-start | bytes 614408 | tf_op jit(solution)/shard_map/ppermute | solution.py:327
  171.1 14.1 %collective-permute-start.21 = (f32[4,72,2560]{2,1,0:T(8,128)}, f32[4,72,2560]{2,1,0:T(8,128)}, u32[]{:S(2)}, u32[]{:S(2)}) collective-permute-start(f32[4,72,2560]{2,1,0:T(8,128)} %ladder.10), channel_id=1, source_target_pairs={{0,1},{1,0},{2,3},{3,2},{4,5},{5,4},{6,7},{7,6},{8,9},{9,8},{10,11... | collective-permute-start | bytes 8847368 | tf_op jit(solution)/shard_map/ppermute | solution.py:409
  173.7 4.4 %collective-permute-start.20 = (f32[136,640]{1,0:T(8,128)S(1)}, f32[136,640]{1,0:T(8,128)S(1)}, u32[]{:S(2)}, u32[]{:S(2)}) collective-permute-start(f32[136,640]{1,0:T(8,128)S(1)} %get-tuple-element.176), channel_id=1, source_target_pairs={{0,1},{1,0},{2,3},{3,2},{4,5},{5,4},{6,7},{7,6},{8,9},{9,8},{10,11... | collective-permute-start | bytes 1044488 | tf_op jit(solution)/shard_map/ppermute | solution.py:334
  179.1 30.9 %collective-permute-start.23 = (f32[272,640]{1,0:T(8,128)}, f32[272,640]{1,0:T(8,128)}, u32[]{:S(2)}, u32[]{:S(2)}) collective-permute-start(f32[272,640]{1,0:T(8,128)} %pad_maximum_fusion.1.refs_0_), channel_id=1, source_target_pairs={{7,5},{6,4},{5,3},{4,2},{3,1},{2,0},{15,13},{14,12},{13,11},{12,10... | collective-permute-start | bytes 2088968 | tf_op jit(solution)/shard_map/ppermute | solution.py:339
  181.0 28.9 %collective-permute-start.22 = (f32[272,640]{1,0:T(8,128)}, f32[272,640]{1,0:T(8,128)}, u32[]{:S(2)}, u32[]{:S(2)}) collective-permute-start(f32[272,640]{1,0:T(8,128)} %pad_maximum_fusion.1.refs_0_), channel_id=1, source_target_pairs={{0,2},{1,3},{2,4},{3,5},{4,6},{5,7},{8,10},{9,11},{10,12},{11,13},... | collective-permute-start | bytes 2088968 | tf_op jit(solution)/shard_map/ppermute | solution.py:339
  209.9 31.0 %copy-start = (f32[4,72,2560]{2,1,0:T(8,128)S(1)}, f32[4,72,2560]{2,1,0:T(8,128)}, u32[]{:S(2)}) copy-start(f32[4,72,2560]{2,1,0:T(8,128)} %ladder.11) | copy-start | bytes 8847364
  212.7 23.0 %collective-permute-start.27 = (f32[72,2560]{1,0:T(8,128)}, f32[72,2560]{1,0:T(8,128)}, u32[]{:S(2)}, u32[]{:S(2)}) collective-permute-start(f32[72,2560]{1,0:T(8,128)} %get-tuple-element.159), channel_id=1, source_target_pairs={{7,5},{6,4},{15,13},{14,12},{23,21},{22,20},{31,29},{30,28}} | collective-permute-start | bytes 2211848 | tf_op jit(solution)/shard_map/ppermute | solution.py:377
  214.0 21.7 %collective-permute-start.26 = (f32[72,2560]{1,0:T(8,128)}, f32[72,2560]{1,0:T(8,128)}, u32[]{:S(2)}, u32[]{:S(2)}) collective-permute-start(f32[72,2560]{1,0:T(8,128)} %get-tuple-element.160), channel_id=1, source_target_pairs={{0,2},{1,3},{8,10},{9,11},{16,18},{17,19},{24,26},{25,27}} | collective-permute-start | bytes 2211848 | tf_op jit(solution)/shard_map/ppermute | solution.py:377
  215.5 18.8 %collective-permute-start.24 = (f32[272,640]{1,0:T(8,128)}, f32[272,640]{1,0:T(8,128)}, u32[]{:S(2)}, u32[]{:S(2)}) collective-permute-start(f32[272,640]{1,0:T(8,128)} %collective-permute-done.22.refs_1_), channel_id=1, source_target_pairs={{2,4},{3,5},{4,6},{5,7},{10,12},{11,13},{12,14},{13,15},{18,20},{1... | collective-permute-start | bytes 2088968 | tf_op jit(solution)/shard_map/ppermute | solution.py:339
  220.4 15.3 %collective-permute-start.25 = (f32[272,640]{1,0:T(8,128)}, f32[272,640]{1,0:T(8,128)}, u32[]{:S(2)}, u32[]{:S(2)}) collective-permute-start(f32[272,640]{1,0:T(8,128)} %collective-permute-done.23.refs_6_), channel_id=1, source_target_pairs={{5,3},{4,2},{3,1},{2,0},{13,11},{12,10},{11,9},{10,8},{21,19},{20,... | collective-permute-start | bytes 2088968 | tf_op jit(solution)/shard_map/ppermute | solution.py:339
  235.7 15.9 %collective-permute-start.28 = (f32[272,640]{1,0:T(8,128)}, f32[272,640]{1,0:T(8,128)}, u32[]{:S(2)}, u32[]{:S(2)}) collective-permute-start(f32[272,640]{1,0:T(8,128)} %collective-permute-done.24.refs_3_), channel_id=1, source_target_pairs={{4,6},{5,7},{12,14},{13,15},{20,22},{21,23},{28,30},{29,31}} | collective-permute-start | bytes 2088968 | tf_op jit(solution)/shard_map/ppermute | solution.py:339
  239.4 12.2 %collective-permute-start.29 = (f32[272,640]{1,0:T(8,128)}, f32[272,640]{1,0:T(8,128)}, u32[]{:S(2)}, u32[]{:S(2)}) collective-permute-start(f32[272,640]{1,0:T(8,128)} %collective-permute-done.25.refs_4_), channel_id=1, source_target_pairs={{3,1},{2,0},{11,9},{10,8},{19,17},{18,16},{27,25},{26,24}} | collective-permute-start | bytes 2088968 | tf_op jit(solution)/shard_map/ppermute | solution.py:339
  243.6 17.8 %collective-permute-start.31 = (f32[72,2560]{1,0:T(8,128)}, f32[72,2560]{1,0:T(8,128)}, u32[]{:S(2)}, u32[]{:S(2)}) collective-permute-start(f32[72,2560]{1,0:T(8,128)} %get-tuple-element.157), channel_id=1, source_target_pairs={{7,5},{6,4},{5,3},{4,2},{15,13},{14,12},{13,11},{12,10},{23,21},{2... | collective-permute-start | bytes 2211848 | tf_op jit(solution)/shard_map/ppermute | solution.py:377
  247.0 17.8 %collective-permute-start.30 = (f32[72,2560]{1,0:T(8,128)}, f32[72,2560]{1,0:T(8,128)}, u32[]{:S(2)}, u32[]{:S(2)}) collective-permute-start(f32[72,2560]{1,0:T(8,128)} %get-tuple-element.158), channel_id=1, source_target_pairs={{0,2},{1,3},{2,4},{3,5},{8,10},{9,11},{10,12},{11,13},{16,18},{17,... | collective-permute-start | bytes 2211848 | tf_op jit(solution)/shard_map/ppermute | solution.py:377
  267.4 29.2 %collective-permute-start.33 = (f32[72,2560]{1,0:T(8,128)}, f32[72,2560]{1,0:T(8,128)}, u32[]{:S(2)}, u32[]{:S(2)}) collective-permute-start(f32[72,2560]{1,0:T(8,128)} %get-tuple-element.155), channel_id=1, source_target_pairs={{7,5},{6,4},{5,3},{4,2},{3,1},{2,0},{15,13},{14,12},{13,11},{12,10... | collective-permute-start | bytes 2211848 | tf_op jit(solution)/shard_map/ppermute | solution.py:377
  269.3 11.8 %copy-start.15 = (f32[64,2560]{1,0:T(8,128)S(1)}, f32[64,2560]{1,0:T(8,128)}, u32[]{:S(2)}) copy-start(f32[64,2560]{1,0:T(8,128)} %reduce-scatter.3.cloned.1.call-done) | copy-start | bytes 1966084
  269.4 11.8 %copy-start.16 = (f32[64,2560]{1,0:T(8,128)S(1)}, f32[64,2560]{1,0:T(8,128)}, u32[]{:S(2)}) copy-start(f32[64,2560]{1,0:T(8,128)} %reduce-scatter.5.cloned.1.call-done) | copy-start | bytes 1966084
  269.4 27.3 %collective-permute-start.32 = (f32[72,2560]{1,0:T(8,128)}, f32[72,2560]{1,0:T(8,128)}, u32[]{:S(2)}, u32[]{:S(2)}) collective-permute-start(f32[72,2560]{1,0:T(8,128)} %get-tuple-element.156), channel_id=1, source_target_pairs={{0,2},{1,3},{2,4},{3,5},{4,6},{5,7},{8,10},{9,11},{10,12},{11,13},... | collective-permute-start | bytes 2211848 | tf_op jit(solution)/shard_map/ppermute | solution.py:377
  283.5 5.4 %collective-permute-start.35 = (f32[32,2560]{1,0:T(8,128)}, f32[32,2560]{1,0:T(8,128)S(1)}, u32[]{:S(2)}, u32[]{:S(2)}) collective-permute-start(f32[32,2560]{1,0:T(8,128)} %get-tuple-element.177), channel_id=1, source_target_pairs={{0,1},{1,0},{2,3},{3,2},{4,5},{5,4},{6,7},{7,6},{8,9},{9,8},{10,11... | collective-permute-start | bytes 983048 | tf_op jit(solution)/shard_map/ppermute | solution.py:444
  288.2 4.9 %collective-permute-start.34 = (f32[32,2560]{1,0:T(8,128)}, f32[32,2560]{1,0:T(8,128)}, u32[]{:S(2)}, u32[]{:S(2)}) collective-permute-start(f32[32,2560]{1,0:T(8,128)} %get-tuple-element.179), channel_id=1, source_target_pairs={{0,1},{1,0},{2,3},{3,2},{4,5},{5,4},{6,7},{7,6},{8,9},{9,8},{10,11... | collective-permute-start | bytes 983048 | tf_op jit(solution)/shard_map/ppermute | solution.py:444
  300.2 1.7 collective-permute-start.36
  302.0 0.7 copy-start.17
  (2 other events, 1.4 us)
Sparse Core Ops, SparseCore 0:
  82.5 53.3 reduce-scatter.2
  138.2 56.2 reduce-scatter.4

commit v2 on v1

--- a/solution.py
+++ b/solution.py
@@ -193,26 +193,26 @@
     )(holes, *loads)
 
 
-def update_kernel(core_ref, driving_ref, denominator_ref, kept_ref, received_ref, *refs):
+def update_kernel(part, core_ref, driving_ref, denominator_ref, kept_ref, received_ref, *refs):
     out_ref = refs[-1]
-    part = kept_ref.shape[1]
-    for half in range(2):
-        lanes = slice(half * part, (half + 1) * part)
-        value = jnp.where(core_ref[0] == half, kept_ref[...], received_ref[...])
+    for number in range(out_ref.shape[1] // part):
+        lanes = slice(number * part, (number + 1) * part)
+        half = slice(number // 2 * part, (number // 2 + 1) * part)
+        value = jnp.where(core_ref[0] == number % 2, kept_ref[:, half], received_ref[:, half])
         out_ref[:, lanes] = (driving_ref[:, lanes] + value) / denominator_ref[:, lanes]
 
 
 def update(core, target, driving, denominator, kept, received, offset, part):
     own, width = driving.shape
     size = min(kept.shape[0], own - offset)
-    tile = next(rows for rows in (32, 16, 8) if offset % rows == 0 and rows <= size)
-    lines = pl.BlockSpec((tile, 2 * part), lambda i, j, core: (offset // tile + i, j))
-    half = pl.BlockSpec((tile, part), lambda i, j, core: (i, j))
+    tile = next(rows for rows in (16, 8) if offset % rows == 0 and rows <= size)
+    lines = pl.BlockSpec((tile, width), lambda i, core: (offset // tile + i, 0))
+    half = pl.BlockSpec((tile, width // 2), lambda i, core: (i, 0))
     return pl.pallas_call(
-        update_kernel,
+        functools.partial(update_kernel, part),
         grid_spec=pltpu.PrefetchScalarGridSpec(
             num_scalar_prefetch=1,
-            grid=(pl.cdiv(size, tile), width // (2 * part)),
+            grid=(pl.cdiv(size, tile),),
             in_specs=[lines, lines, half, half] + [pl.BlockSpec(memory_space=pl.ANY)] * len(target),
             out_specs=lines,
         ),

time: 316 us -> 311 us (0.984)
  Pallas kernels: 153 us -> 148 us
    pallas_call x3, Pallas kernels: 12.6 us -> 7.65 us  [update(): pl.pallas_call(functools.partial(update_kernel, part), grid_spec=pltpu.Pr...]
where the time goes in v2:
time: 311 us; the launch traced here: 310 us
  Pallas kernels  148 us (48%)
  starting transfers between devices  56.9 us (18%)
  waiting for transfers between devices  51.8 us (17%)
  local copies, waits for them, and re-layouts  21.6 us (7%)
  other arithmetic  18 us (6%)
  between operations  14 us (5%)
    pallas_call x6, Pallas kernels, ladder(): pl.pallas_call(functools.partial(ladder_kernel, len(pieces)), grid_spec=p...  120 us
    ppermute x3, waiting for transfers between devices, exchange_segments(): lax.ppermute(right[-1], 'col', up)  13.6 us
    ppermute x3, starting transfers between devices, exchange_segments(): lax.ppermute(right[-1], 'col', up)  12.8 us
    ppermute x3, waiting for transfers between devices, walk_line(): lax.ppermute(to_left, 'col', down)  9.78 us
    pallas_call x3, Pallas kernels, update(): pl.pallas_call(functools.partial(update_kernel, part), grid_spec=pltpu.Pr...  7.65 us
    ppermute x3, starting transfers between devices, walk_line(): lax.ppermute(to_right, 'col', up)  7.42 us
    pallas_call x1, Pallas kernels, spread(): pl.pallas_call(functools.partial(spread_kernel, count), grid=(segments,),...  7.4 us
    squeeze x5, local copies, waits for them, and re-layouts, at(): return lax.dynamic_index_in_dim(array, index, 0, keepdims=False)  7.39 us
  transfers between devices with their start and end apart: 39, of which 14 were waited for; matrix products, arithmetic and copies ran while one was open for 8% of the time, Pallas kernels for 47%

profile of v2, /device:TPU:21, one launch (start us, length us, event | category | flops | bytes accessed | tf_op | source)
XLA Modules:
  0.0 310.1 jit_solution(4005425218075576241)
XLA Ops:
  6.5 1.8 reshape.421
  8.8 1.2 collective-permute-start
  11.6 2.5 fusion.12
  14.6 2.6 fusion.13
  17.4 1.2 reshape.424.refs_10_.refs_0_
  18.9 5.3 %collective-permute-done.1.refs_2_ = f32[64,2560]{1,0:T(8,128)} collective-permute-done((f32[64,2560]{1,0:T(8,128)S(1)}, f32[64,2560]{1,0:T(8,128)}, u32[]{:S(2)}, u32[]{:S(2)}) %collective-permute-start.1) | collective-permute-done | bytes 655392 | tf_op jit(solution)/shard_map/ppermute | solution.py:267
  25.3 1.3 collective-permute-start.2
  26.5 1.0 slice.83
  29.4 3.5 %collective-permute-done.2.refs_3_ = f32[32,2560]{1,0:T(8,128)S(1)} collective-permute-done((f32[32,2560]{1,0:T(8,128)S(1)}, f32[32,2560]{1,0:T(8,128)S(1)}, u32[]{:S(2)}, u32[]{:S(2)}) %collective-permute-start.2) | collective-permute-done | bytes 327712 | tf_op jit(solution)/shard_map/ppermute | solution.py:273
  33.0 2.0 collective-permute-done.3.refs_4_
  35.7 17.4 %ladder.6 = f32[4,64,2560]{2,1,0:T(8,128)} custom-call(s32[2]{0:T(128)} %get-tuple-element.123.where_ref, f32[64,2560]{1,0:T(8,128)} %bitcast.101, f32[64,2560]{1,0:T(8,128)} %collective-permute-done.refs_1_, f32[64,2560]{1,0:T(8,128)} %collective-permute-done.1.refs_2_, f32[32,2560]{1,0:T(8,128)} %copy-done.9, f32[32,2560]{1,0:T(8,128)} %copy-done.10, ...), custom_call_target="tpu_custom_call" | custom-call | flops 1677721600 | bytes 1638400 | tf_op jit(solution)/shard_map/ladder/pallas_call | solution.py:62
  53.2 3.1 %collective-permute-start.6 = (f32[4,64,2560]{2,1,0:T(8,128)}, f32[4,64,2560]{2,1,0:T(8,128)S(1)}, u32[]{:S(2)}, u32[]{:S(2)}) collective-permute-start(f32[4,64,2560]{2,1,0:T(8,128)} %ladder.6), channel_id=1, source_target_pairs={{0,1},{1,0},{2,3},{3,2},{4,5},{5,4},{6,7},{7,6},{8,9},{9,8},{10,11... | collective-permute-start | bytes 7864328 | tf_op jit(solution)/shard_map/ppermute | solution.py:409
  56.3 1.3 collective-permute-start.10
  57.5 1.2 collective-permute-start.9
  59.4 1.7 collective-permute-done.6.refs_6_
  61.0 1.5 copy-done.14
  62.5 17.8 %ladder.7 = f32[4,64,2560]{2,1,0:T(8,128)} custom-call(s32[2]{0:T(128)} %get-tuple-element.130.where_ref, f32[64,2560]{1,0:T(8,128)} %bitcast.102, f32[64,2560]{1,0:T(8,128)} %collective-permute-done.refs_1_, f32[64,2560]{1,0:T(8,128)} %collective-permute-done.1.refs_2_, f32[32,2560]{1,0:T(8,128)} %copy-done.9, f32[32,2560]{1,0:T(8,128)} %copy-done.10, ...), custom_call_target="tpu_custom_call" | custom-call | flops 1677721600 | bytes 1638400 | tf_op jit(solution)/shard_map/ladder/pallas_call | solution.py:62
  80.3 2.0 collective-permute-done.7.refs_3_.refs_8_
  83.0 1.3 collective-permute-start.11
  84.3 17.6 %ladder.8 = f32[4,64,2560]{2,1,0:T(8,128)} custom-call(s32[2]{0:T(128)} %get-tuple-element.123.where_ref, f32[64,2560]{1,0:T(8,128)} %bitcast.96, f32[64,2560]{1,0:T(8,128)} %copy-done.7, f32[64,2560]{1,0:T(8,128)} %copy-done.6, f32[32,2560]{1,0:T(8,128)} %copy-done.11, f32[32,2560]{1,0:T(8,128)} %copy-done.12, f32[5120,2560]{1,0:T(8,128)} %refs_5_.11), custom_call_target="tpu_custom_call" | custom-call | flops 1677721600 | bytes 1638400 | tf_op jit(solution)/shard_map/ladder/pallas_call | solution.py:62
  101.9 1.6 collective-permute-start.13
  104.3 6.4 %pick.1 = f32[4,40,1280]{2,1,0:T(8,128)} custom-call(s32[160,1]{1,0:T(8,128)} %get-tuple-element.79.place_ref, s32[160,1]{1,0:T(8,128)} %get-tuple-element.80.segment_ref, f32[160,1]{1,0:T(8,128)} %copy.25.factor_ref, f32[64,2560]{1,0:T(8,128)} %bitcast.103, f32[64,2560]{1,0:T(8,128)} %collective-permute-done.refs_1_, ...), custom_call_target="tpu_custom_call" | custom-call | flops 204800 | bytes 204800 | tf_op jit(solution)/shard_map/pick/pallas_call | solution.py:109
  110.7 2.0 dynamic-slice_bitcast_fusion.8
  112.7 1.2 collective-permute-start.16
  114.1 1.2 collective-permute-start.14
  115.3 17.8 %ladder.9 = f32[4,64,2560]{2,1,0:T(8,128)} custom-call(s32[2]{0:T(128)} %get-tuple-element.130.where_ref, f32[64,2560]{1,0:T(8,128)} %bitcast.98, f32[64,2560]{1,0:T(8,128)} %copy-done.7, f32[64,2560]{1,0:T(8,128)} %copy-done.6, f32[32,2560]{1,0:T(8,128)} %copy-done.11, f32[32,2560]{1,0:T(8,128)} %copy-done.12, f32[5120,2560]{1,0:T(8,128)} %refs_5_.11, ...), custom_call_target="tpu_custom_call" | custom-call | flops 1677721600 | bytes 1638400 | tf_op jit(solution)/shard_map/ladder/pallas_call | solution.py:62
  133.2 2.7 reduce-scatter.3.cloned.1.call-done
  136.0 6.5 %mix.1 = f32[4,40,1280]{2,1,0:T(8,128)} custom-call(f32[1280,1280]{1,0:T(8,128)} %bitcast.106, f32[40,1280]{1,0:T(8,128)} %get-tuple-element.118.refs_0_, f32[40,1280]{1,0:T(8,128)} %copy-done.21, f32[40,1280]{1,0:T(8,128)} %copy-done.20, f32[40,1280]{1,0:T(8,128)} %copy-done.19), custom_call_target="tpu_custom_call" | custom-call | flops 1572864000 | bytes 8192000 | tf_op jit(solution)/shard_map/mix/pallas_call | solution.py:132
  142.5 1.3 slice_bitcast_fusion
  143.8 1.2 collective-permute-start.19
  145.0 1.2 collective-permute-start.18
  146.5 24.5 %ladder.10 = f32[4,72,2560]{2,1,0:T(8,128)} custom-call(s32[2]{0:T(128)} %get-tuple-element.123.where_ref, f32[72,2560]{1,0:T(8,128)} %copy-done.1, f32[72,2560]{1,0:T(8,128)} %copy-done.4, f32[72,2560]{1,0:T(8,128)} %copy-done.5, f32[32,2560]{1,0:T(8,128)} %copy-done.13, f32[40,2560]{1,0:T(8,128)} %copy-done.8, f32[5120,2560]{1,0:T(8,128)} %refs_5_.11), custom_call_target="tpu_custom_call" | custom-call | flops 1887436800 | bytes 1638400 | tf_op jit(solution)/shard_map/ladder/pallas_call | solution.py:62
  171.1 1.6 collective-permute-start.21
  173.8 4.3 %collective-permute-done.20 = f32[136,640]{1,0:T(8,128)S(1)} collective-permute-done((f32[136,640]{1,0:T(8,128)S(1)}, f32[136,640]{1,0:T(8,128)S(1)}, u32[]{:S(2)}, u32[]{:S(2)}) %collective-permute-start.20) | collective-permute-done | bytes 348192 | tf_op jit(solution)/shard_map/ppermute | solution.py:334
  179.1 1.9 collective-permute-start.23
  181.0 4.2 %collective-permute-start.22 = (f32[272,640]{1,0:T(8,128)}, f32[272,640]{1,0:T(8,128)}, u32[]{:S(2)}, u32[]{:S(2)}) collective-permute-start(f32[272,640]{1,0:T(8,128)} %pad_maximum_fusion.1.refs_0_), channel_id=1, source_target_pairs={{0,2},{1,3},{2,4},{3,5},{4,6},{5,7},{8,10},{9,11},{10,12},{11,13},... | collective-permute-start | bytes 2088968 | tf_op jit(solution)/shard_map/ppermute | solution.py:339
  185.2 24.7 %ladder.11 = f32[4,72,2560]{2,1,0:T(8,128)} custom-call(s32[2]{0:T(128)} %get-tuple-element.130.where_ref, f32[72,2560]{1,0:T(8,128)} %copy-done.1, f32[72,2560]{1,0:T(8,128)} %copy-done.4, f32[72,2560]{1,0:T(8,128)} %copy-done.5, f32[32,2560]{1,0:T(8,128)} %copy-done.13, f32[40,2560]{1,0:T(8,128)} %copy-done.8, f32[5120,2560]{1,0:T(8,128)} %refs_5_.11, ...), custom_call_target="tpu_custom_call" | custom-call | flops 1887436800 | bytes 1638400 | tf_op jit(solution)/shard_map/ladder/pallas_call | solution.py:62
  209.9 2.8 dynamic-slice_bitcast_fusion
  212.7 1.3 collective-permute-start.27
  214.0 1.5 collective-permute-start.26
  215.5 4.8 %collective-permute-start.24 = (f32[272,640]{1,0:T(8,128)}, f32[272,640]{1,0:T(8,128)}, u32[]{:S(2)}, u32[]{:S(2)}) collective-permute-start(f32[272,640]{1,0:T(8,128)} %collective-permute-done.22.refs_1_), channel_id=1, source_target_pairs={{2,4},{3,5},{4,6},{5,7},{10,12},{11,13},{12,14},{13,15},{18,20},{1... | collective-permute-start | bytes 2088968 | tf_op jit(solution)/shard_map/ppermute | solution.py:339
  220.4 2.2 collective-permute-start.25
  222.5 11.8 %collective-permute-done.24.refs_3_ = f32[272,640]{1,0:T(8,128)} collective-permute-done((f32[272,640]{1,0:T(8,128)}, f32[272,640]{1,0:T(8,128)}, u32[]{:S(2)}, u32[]{:S(2)}) %collective-permute-start.24) | collective-permute-done | bytes 696352 | tf_op jit(solution)/shard_map/ppermute | solution.py:339
  234.4 1.3 collective-permute-done.25.refs_4_
  235.7 3.7 %collective-permute-start.28 = (f32[272,640]{1,0:T(8,128)}, f32[272,640]{1,0:T(8,128)}, u32[]{:S(2)}, u32[]{:S(2)}) collective-permute-start(f32[272,640]{1,0:T(8,128)} %collective-permute-done.24.refs_3_), channel_id=1, source_target_pairs={{4,6},{5,7},{12,14},{13,15},{20,22},{21,23},{28,30},{29,31}} | collective-permute-start | bytes 2088968 | tf_op jit(solution)/shard_map/ppermute | solution.py:339
  239.4 1.5 collective-permute-start.29
  240.9 2.6 bitcast_add_fusion.1
  243.6 3.5 %collective-permute-start.31 = (f32[72,2560]{1,0:T(8,128)}, f32[72,2560]{1,0:T(8,128)}, u32[]{:S(2)}, u32[]{:S(2)}) collective-permute-start(f32[72,2560]{1,0:T(8,128)} %get-tuple-element.157), channel_id=1, source_target_pairs={{7,5},{6,4},{5,3},{4,2},{15,13},{14,12},{13,11},{12,10},{23,21},{2... | collective-permute-start | bytes 2211848 | tf_op jit(solution)/shard_map/ppermute | solution.py:377
  247.0 1.6 collective-permute-start.30
  249.7 1.8 collective-permute-done.28.refs_5_
  251.6 9.8 %collective-permute-done.31 = f32[72,2560]{1,0:T(8,128)} collective-permute-done((f32[72,2560]{1,0:T(8,128)}, f32[72,2560]{1,0:T(8,128)}, u32[]{:S(2)}, u32[]{:S(2)}) %collective-permute-start.31) | collective-permute-done | bytes 737312 | tf_op jit(solution)/shard_map/ppermute | solution.py:377
  261.3 3.5 %collective-permute-done.30 = f32[72,2560]{1,0:T(8,128)} collective-permute-done((f32[72,2560]{1,0:T(8,128)}, f32[72,2560]{1,0:T(8,128)}, u32[]{:S(2)}, u32[]{:S(2)}) %collective-permute-start.30) | collective-permute-done | bytes 737312 | tf_op jit(solution)/shard_map/ppermute | solution.py:377
  264.8 2.6 bitcast_add_fusion
  267.4 1.9 collective-permute-start.33
  269.4 4.3 %collective-permute-start.32 = (f32[72,2560]{1,0:T(8,128)}, f32[72,2560]{1,0:T(8,128)}, u32[]{:S(2)}, u32[]{:S(2)}) collective-permute-start(f32[72,2560]{1,0:T(8,128)} %get-tuple-element.156), channel_id=1, source_target_pairs={{0,2},{1,3},{2,4},{3,5},{4,6},{5,7},{8,10},{9,11},{10,12},{11,13},... | collective-permute-start | bytes 2211848 | tf_op jit(solution)/shard_map/ppermute | solution.py:377
  273.7 7.4 %spread.1 = f32[200,2560]{1,0:T(8,128)} custom-call(s32[200,1]{1,0:T(8,128)} %copy.26.holes_ref, f32[272,640]{1,0:T(8,128)} %pad_maximum_fusion.1.refs_0_, f32[272,640]{1,0:T(8,128)} %collective-permute-done.22.refs_1_, f32[272,640]{1,0:T(8,128)} %collective-permute-done.29.refs_2_, f32[272,640]{1,0:T(8,128)} %collective-permute-done.24.refs_3_, ...), custom_call_target="tpu_custom_call" | custom-call | flops 512000 | bytes 512000 | tf_op jit(solution)/shard_map/spread/pallas_call | solution.py:178
  281.1 1.4 slice_add_fusion.1
  283.5 3.9 %collective-permute-start.35 = (f32[32,2560]{1,0:T(8,128)}, f32[32,2560]{1,0:T(8,128)S(1)}, u32[]{:S(2)}, u32[]{:S(2)}) collective-permute-start(f32[32,2560]{1,0:T(8,128)} %get-tuple-element.177), channel_id=1, source_target_pairs={{0,1},{1,0},{2,3},{3,2},{4,5},{5,4},{6,7},{7,6},{8,9},{9,8},{10,11... | collective-permute-start | bytes 983048 | tf_op jit(solution)/shard_map/ppermute | solution.py:444
  289.5 2.2 update.3.refs_0_
  291.8 2.3 update.4.refs_0_
  294.0 1.5 fusion
  295.5 1.2 slice_add_fusion
  298.0 1.4 collective-permute-done.36.received_ref
  300.1 3.1 %update.5 = f32[100,5120]{1,0:T(8,128)} custom-call(s32[1]{0:T(128)} %bitcast.core_ref, f32[100,5120]{1,0:T(8,128)} %driving_ref.5, f32[100,5120]{1,0:T(8,128)} %denominator_ref.5, f32[36,2560]{1,0:T(8,128)} %get-tuple-element.166.kept_ref, f32[36,2560]{1,0:T(8,128)} %copy-done.17, f32[100,5120]{1,0:T(8,128)} %update.4.refs_0_), custom_call_target="tpu_custom_call", output_to_operand_aliasing={{}: (5, {})} | custom-call | flops 184320 | bytes 184320 | tf_op jit(solution)/shard_map/update/pallas_call | solution.py:211
  (136 shorter events, 17.6 us)
Async XLA Ops:
  6.5 129.4 %reduce-scatter.3.cloned.1.call-start = ((), (), s32[]{:S(2)}) async-start(), calls=%async_computation.2 | async-start | bytes 3276800 | tf_op jit(solution)/shard_map/reduce_scatter | solution.py:358
  8.3 2.6 copy-start.26
  8.3 2.6 copy-start.22
  8.3 3.3 %copy-start.23 = (s32[1,128,1]{1,2,0:T(1,128)S(1)}, s32[1,128,1]{1,2,0:T(1,128)}, u32[]{:S(2)}) copy-start(s32[1,128,1]{1,2,0:T(1,128)} %param.14) | copy-start | bytes 1540
  8.4 8.8 %copy-start.24 = (s32[1,128]{1,0:T(1,128)S(1)}, s32[1,128]{1,0:T(1,128)}, u32[]{:S(2)}) copy-start(s32[1,128]{1,0:T(1,128)} %param.15) | copy-start | bytes 1540
  8.4 10.5 %copy-start.25 = (f32[1,128]{1,0:T(1,128)S(1)}, f32[1,128]{1,0:T(1,128)}, u32[]{:S(2)}) copy-start(f32[1,128]{1,0:T(1,128)} %param.17) | copy-start | bytes 1540
  8.5 27.0 %copy-start.3 = (f32[2,32,2560]{2,1,0:T(8,128)}, f32[2,32,2560]{2,1,0:T(8,128)S(1)}, u32[]{:S(2)}) copy-start(f32[2,32,2560]{2,1,0:T(8,128)S(1)} %get-tuple-element.162) | copy-start | bytes 1966084
  8.5 44.6 %copy-start.2 = (f32[2,32,2560]{2,1,0:T(8,128)}, f32[2,32,2560]{2,1,0:T(8,128)S(1)}, u32[]{:S(2)}) copy-start(f32[2,32,2560]{2,1,0:T(8,128)S(1)} %get-tuple-element.161) | copy-start | bytes 1966084
  8.5 15.8 %collective-permute-start.1 = (f32[64,2560]{1,0:T(8,128)S(1)}, f32[64,2560]{1,0:T(8,128)}, u32[]{:S(2)}, u32[]{:S(2)}) collective-permute-start(f32[64,2560]{1,0:T(8,128)S(1)} %bitcast.99), channel_id=1, source_target_pairs={{0,16},{8,24},{16,0},{24,8},{1,17},{9,25},{17,1},{25,9},{2,18},{10... | collective-permute-start | bytes 1966088 | tf_op jit(solution)/shard_map/ppermute | solution.py:267
  8.8 17.8 %collective-permute-start = (f32[64,2560]{1,0:T(8,128)S(1)}, f32[64,2560]{1,0:T(8,128)}, u32[]{:S(2)}, u32[]{:S(2)}) collective-permute-start(f32[64,2560]{1,0:T(8,128)S(1)} %bitcast.100), channel_id=1, source_target_pairs={{0,8},{8,0},{16,24},{24,16},{1,9},{9,1},{17,25},{25,17},{2,10},{10... | collective-permute-start | bytes 1966088 | tf_op jit(solution)/shard_map/ppermute | solution.py:267
  18.7 38.9 %copy-start.1 = (f32[72,2560]{1,0:T(8,128)}, f32[72,2560]{1,0:T(8,128)S(1)}, u32[]{:S(2)}) copy-start(f32[72,2560]{1,0:T(8,128)S(1)} %reshape.424.refs_10_.refs_0_) | copy-start | bytes 2211844
  25.3 7.7 %collective-permute-start.2 = (f32[32,2560]{1,0:T(8,128)S(1)}, f32[32,2560]{1,0:T(8,128)S(1)}, u32[]{:S(2)}, u32[]{:S(2)}) collective-permute-start(f32[32,2560]{1,0:T(8,128)S(1)} %slice.82), channel_id=1, source_target_pairs={{0,8},{8,0},{16,24},{24,16},{1,9},{9,1},{17,25},{25,17},{2,10},{10... | collective-permute-start | bytes 983048 | tf_op jit(solution)/shard_map/ppermute | solution.py:273
  27.5 7.4 %collective-permute-start.3 = (f32[32,2560]{1,0:T(8,128)S(1)}, f32[32,2560]{1,0:T(8,128)S(1)}, u32[]{:S(2)}, u32[]{:S(2)}) collective-permute-start(f32[32,2560]{1,0:T(8,128)S(1)} %slice.83), channel_id=1, source_target_pairs={{0,16},{8,24},{16,0},{24,8},{1,17},{9,25},{17,1},{25,9},{2,18},{10... | collective-permute-start | bytes 983048 | tf_op jit(solution)/shard_map/ppermute | solution.py:274
  33.0 2.5 copy-start.9
  35.0 18.1 %collective-permute-start.5 = (f32[64,2560]{1,0:T(8,128)S(1)}, f32[64,2560]{1,0:T(8,128)S(1)}, u32[]{:S(2)}, u32[]{:S(2)}) collective-permute-start(f32[64,2560]{1,0:T(8,128)S(1)} %bitcast.94), channel_id=1, source_target_pairs={{0,16},{8,24},{16,0},{24,8},{1,17},{9,25},{17,1},{25,9},{2,18},{10... | collective-permute-start | bytes 1966088 | tf_op jit(solution)/shard_map/ppermute | solution.py:267
  35.2 17.9 %collective-permute-start.4 = (f32[64,2560]{1,0:T(8,128)S(1)}, f32[64,2560]{1,0:T(8,128)S(1)}, u32[]{:S(2)}, u32[]{:S(2)}) collective-permute-start(f32[64,2560]{1,0:T(8,128)S(1)} %bitcast.95), channel_id=1, source_target_pairs={{0,8},{8,0},{16,24},{24,16},{1,9},{9,1},{17,25},{25,17},{2,10},{10... | collective-permute-start | bytes 1966088 | tf_op jit(solution)/shard_map/ppermute | solution.py:267
  53.1 27.2 %copy-start.6 = (f32[64,2560]{1,0:T(8,128)}, f32[64,2560]{1,0:T(8,128)S(1)}, u32[]{:S(2)}) copy-start(f32[64,2560]{1,0:T(8,128)S(1)} %collective-permute-done.5.refs_2_.refs_7_) | copy-start | bytes 1966084
  53.2 27.1 %copy-start.7 = (f32[64,2560]{1,0:T(8,128)}, f32[64,2560]{1,0:T(8,128)S(1)}, u32[]{:S(2)}) copy-start(f32[64,2560]{1,0:T(8,128)S(1)} %collective-permute-done.4.refs_1_.refs_6_) | copy-start | bytes 1966084
  53.2 7.9 %collective-permute-start.6 = (f32[4,64,2560]{2,1,0:T(8,128)}, f32[4,64,2560]{2,1,0:T(8,128)S(1)}, u32[]{:S(2)}, u32[]{:S(2)}) collective-permute-start(f32[4,64,2560]{2,1,0:T(8,128)} %ladder.6), channel_id=1, source_target_pairs={{0,1},{1,0},{2,3},{3,2},{4,5},{5,4},{6,7},{7,6},{8,9},{9,8},{10,11... | collective-permute-start | bytes 7864328 | tf_op jit(solution)/shard_map/ppermute | solution.py:409
  56.3 26.0 %collective-permute-start.10 = (f32[72,2560]{1,0:T(8,128)S(1)}, f32[72,2560]{1,0:T(8,128)S(1)}, u32[]{:S(2)}, u32[]{:S(2)}) collective-permute-start(f32[72,2560]{1,0:T(8,128)S(1)} %reshape.424.refs_10_.refs_0_), channel_id=1, source_target_pairs={{0,16},{8,24},{16,0},{24,8},{1,17},{9,25},{17,1},{25,9},{2,18},{10... | collective-permute-start | bytes 2211848 | tf_op jit(solution)/shard_map/ppermute | solution.py:267
  57.5 24.8 %collective-permute-start.9 = (f32[72,2560]{1,0:T(8,128)S(1)}, f32[72,2560]{1,0:T(8,128)S(1)}, u32[]{:S(2)}, u32[]{:S(2)}) collective-permute-start(f32[72,2560]{1,0:T(8,128)S(1)} %reshape.424.refs_10_.refs_0_), channel_id=1, source_target_pairs={{0,8},{8,0},{16,24},{24,16},{1,9},{9,1},{17,25},{25,17},{2,10},{10... | collective-permute-start | bytes 2211848 | tf_op jit(solution)/shard_map/ppermute | solution.py:267
  58.8 23.5 %collective-permute-start.7 = (f32[32,2560]{1,0:T(8,128)S(1)}, f32[32,2560]{1,0:T(8,128)S(1)}, u32[]{:S(2)}, u32[]{:S(2)}) collective-permute-start(f32[32,2560]{1,0:T(8,128)S(1)} %slice.59), channel_id=1, source_target_pairs={{0,8},{8,0},{16,24},{24,16},{1,9},{9,1},{17,25},{25,17},{2,10},{10... | collective-permute-start | bytes 983048 | tf_op jit(solution)/shard_map/ppermute | solution.py:273
  59.1 23.2 %collective-permute-start.8 = (f32[32,2560]{1,0:T(8,128)S(1)}, f32[32,2560]{1,0:T(8,128)S(1)}, u32[]{:S(2)}, u32[]{:S(2)}) collective-permute-start(f32[32,2560]{1,0:T(8,128)S(1)} %slice.60), channel_id=1, source_target_pairs={{0,16},{8,24},{16,0},{24,8},{1,17},{9,25},{17,1},{25,9},{2,18},{10... | collective-permute-start | bytes 983048 | tf_op jit(solution)/shard_map/ppermute | solution.py:274
  61.0 1.5 copy-start.14
  82.3 2.0 copy-start.11
  82.3 2.0 copy-start.12
  82.3 19.6 %copy-start.5 = (f32[72,2560]{1,0:T(8,128)}, f32[72,2560]{1,0:T(8,128)S(1)}, u32[]{:S(2)}) copy-start(f32[72,2560]{1,0:T(8,128)S(1)} %collective-permute-done.10.refs_12_.refs_2_) | copy-start | bytes 2211844
  82.3 19.6 %copy-start.4 = (f32[72,2560]{1,0:T(8,128)}, f32[72,2560]{1,0:T(8,128)S(1)}, u32[]{:S(2)}) copy-start(f32[72,2560]{1,0:T(8,128)S(1)} %collective-permute-done.9.refs_11_.refs_1_) | copy-start | bytes 2211844
  82.4 127.6 %reduce-scatter.5.cloned.1.call-start = ((), (), s32[]{:S(2)}) async-start(), calls=%async_computation.3 | async-start | bytes 3276800 | tf_op jit(solution)/shard_map/reduce_scatter | solution.py:358
  82.6 19.3 %collective-permute-start.12 = (f32[40,2560]{1,0:T(8,128)S(1)}, f32[40,2560]{1,0:T(8,128)S(1)}, u32[]{:S(2)}, u32[]{:S(2)}) collective-permute-start(f32[40,2560]{1,0:T(8,128)S(1)} %slice.62), channel_id=1, source_target_pairs={{0,16},{8,24},{16,0},{24,8},{1,17},{9,25},{17,1},{25,9},{2,18},{10... | collective-permute-start | bytes 1228808 | tf_op jit(solution)/shard_map/ppermute | solution.py:274
  83.0 18.9 %collective-permute-start.11 = (f32[32,2560]{1,0:T(8,128)S(1)}, f32[32,2560]{1,0:T(8,128)S(1)}, u32[]{:S(2)}, u32[]{:S(2)}) collective-permute-start(f32[32,2560]{1,0:T(8,128)S(1)} %slice.61), channel_id=1, source_target_pairs={{0,8},{8,0},{16,24},{24,16},{1,9},{9,1},{17,25},{25,17},{2,10},{10... | collective-permute-start | bytes 983048 | tf_op jit(solution)/shard_map/ppermute | solution.py:273
  101.9 2.4 copy-start.13
  101.9 2.4 copy-start.8
  101.9 13.4 %collective-permute-start.13 = (f32[4,64,2560]{2,1,0:T(8,128)}, f32[4,64,2560]{2,1,0:T(8,128)}, u32[]{:S(2)}, u32[]{:S(2)}) collective-permute-start(f32[4,64,2560]{2,1,0:T(8,128)} %ladder.8), channel_id=1, source_target_pairs={{0,1},{1,0},{2,3},{3,2},{4,5},{5,4},{6,7},{7,6},{8,9},{9,8},{10,11... | collective-permute-start | bytes 7864328 | tf_op jit(solution)/shard_map/ppermute | solution.py:409
  112.7 20.5 %collective-permute-start.16 = (f32[40,1280]{1,0:T(8,128)S(1)}, f32[40,1280]{1,0:T(8,128)S(1)}, u32[]{:S(2)}, u32[]{:S(2)}) collective-permute-start(f32[40,1280]{1,0:T(8,128)S(1)} %get-tuple-element.171), channel_id=1, source_target_pairs={{0,24},{8,16},{16,8},{24,0},{1,25},{9,17},{17,9},{25,1},{2,26},{10... | collective-permute-start | bytes 614408 | tf_op jit(solution)/shard_map/ppermute | solution.py:323
  113.9 19.3 %collective-permute-start.15 = (f32[40,1280]{1,0:T(8,128)S(1)}, f32[40,1280]{1,0:T(8,128)S(1)}, u32[]{:S(2)}, u32[]{:S(2)}) collective-permute-start(f32[40,1280]{1,0:T(8,128)S(1)} %get-tuple-element.172), channel_id=1, source_target_pairs={{0,16},{8,24},{16,0},{24,8},{1,17},{9,25},{17,1},{25,9},{2,18},{10... | collective-permute-start | bytes 614408 | tf_op jit(solution)/shard_map/ppermute | solution.py:323
  114.1 19.1 %collective-permute-start.14 = (f32[40,1280]{1,0:T(8,128)S(1)}, f32[40,1280]{1,0:T(8,128)S(1)}, u32[]{:S(2)}, u32[]{:S(2)}) collective-permute-start(f32[40,1280]{1,0:T(8,128)S(1)} %get-tuple-element.173), channel_id=1, source_target_pairs={{0,8},{8,0},{16,24},{24,16},{1,9},{9,1},{17,25},{25,17},{2,10},{10... | collective-permute-start | bytes 614408 | tf_op jit(solution)/shard_map/ppermute | solution.py:323
  133.2 2.8 copy-start.19
  133.2 2.8 copy-start.20
  133.2 2.8 copy-start.21
  143.8 27.3 %collective-permute-start.19 = (f32[40,1280]{1,0:T(8,128)S(1)}, f32[40,1280]{1,0:T(8,128)S(1)}, u32[]{:S(2)}, u32[]{:S(2)}) collective-permute-start(f32[40,1280]{1,0:T(8,128)S(1)} %get-tuple-element.167), channel_id=1, source_target_pairs={{0,24},{8,16},{16,8},{24,0},{1,25},{9,17},{17,9},{25,1},{2,26},{10... | collective-permute-start | bytes 614408 | tf_op jit(solution)/shard_map/ppermute | solution.py:327
  145.0 26.1 %collective-permute-start.18 = (f32[40,1280]{1,0:T(8,128)S(1)}, f32[40,1280]{1,0:T(8,128)S(1)}, u32[]{:S(2)}, u32[]{:S(2)}) collective-permute-start(f32[40,1280]{1,0:T(8,128)S(1)} %get-tuple-element.168), channel_id=1, source_target_pairs={{0,16},{8,24},{16,0},{24,8},{1,17},{9,25},{17,1},{25,9},{2,18},{10... | collective-permute-start | bytes 614408 | tf_op jit(solution)/shard_map/ppermute | solution.py:327
  146.2 24.8 %collective-permute-start.17 = (f32[40,1280]{1,0:T(8,128)S(1)}, f32[40,1280]{1,0:T(8,128)S(1)}, u32[]{:S(2)}, u32[]{:S(2)}) collective-permute-start(f32[40,1280]{1,0:T(8,128)S(1)} %get-tuple-element.169), channel_id=1, source_target_pairs={{0,8},{8,0},{16,24},{24,16},{1,9},{9,1},{17,25},{25,17},{2,10},{10... | collective-permute-start | bytes 614408 | tf_op jit(solution)/shard_map/ppermute | solution.py:327
  171.1 14.1 %collective-permute-start.21 = (f32[4,72,2560]{2,1,0:T(8,128)}, f32[4,72,2560]{2,1,0:T(8,128)}, u32[]{:S(2)}, u32[]{:S(2)}) collective-permute-start(f32[4,72,2560]{2,1,0:T(8,128)} %ladder.10), channel_id=1, source_target_pairs={{0,1},{1,0},{2,3},{3,2},{4,5},{5,4},{6,7},{7,6},{8,9},{9,8},{10,11... | collective-permute-start | bytes 8847368 | tf_op jit(solution)/shard_map/ppermute | solution.py:409
  173.7 4.4 %collective-permute-start.20 = (f32[136,640]{1,0:T(8,128)S(1)}, f32[136,640]{1,0:T(8,128)S(1)}, u32[]{:S(2)}, u32[]{:S(2)}) collective-permute-start(f32[136,640]{1,0:T(8,128)S(1)} %get-tuple-element.176), channel_id=1, source_target_pairs={{0,1},{1,0},{2,3},{3,2},{4,5},{5,4},{6,7},{7,6},{8,9},{9,8},{10,11... | collective-permute-start | bytes 1044488 | tf_op jit(solution)/shard_map/ppermute | solution.py:334
  179.1 30.9 %collective-permute-start.23 = (f32[272,640]{1,0:T(8,128)}, f32[272,640]{1,0:T(8,128)}, u32[]{:S(2)}, u32[]{:S(2)}) collective-permute-start(f32[272,640]{1,0:T(8,128)} %pad_maximum_fusion.1.refs_0_), channel_id=1, source_target_pairs={{7,5},{6,4},{5,3},{4,2},{3,1},{2,0},{15,13},{14,12},{13,11},{12,10... | collective-permute-start | bytes 2088968 | tf_op jit(solution)/shard_map/ppermute | solution.py:339
  181.0 28.9 %collective-permute-start.22 = (f32[272,640]{1,0:T(8,128)}, f32[272,640]{1,0:T(8,128)}, u32[]{:S(2)}, u32[]{:S(2)}) collective-permute-start(f32[272,640]{1,0:T(8,128)} %pad_maximum_fusion.1.refs_0_), channel_id=1, source_target_pairs={{0,2},{1,3},{2,4},{3,5},{4,6},{5,7},{8,10},{9,11},{10,12},{11,13},... | collective-permute-start | bytes 2088968 | tf_op jit(solution)/shard_map/ppermute | solution.py:339
  209.9 31.0 %copy-start = (f32[4,72,2560]{2,1,0:T(8,128)S(1)}, f32[4,72,2560]{2,1,0:T(8,128)}, u32[]{:S(2)}) copy-start(f32[4,72,2560]{2,1,0:T(8,128)} %ladder.11) | copy-start | bytes 8847364
  212.7 23.0 %collective-permute-start.27 = (f32[72,2560]{1,0:T(8,128)}, f32[72,2560]{1,0:T(8,128)}, u32[]{:S(2)}, u32[]{:S(2)}) collective-permute-start(f32[72,2560]{1,0:T(8,128)} %get-tuple-element.159), channel_id=1, source_target_pairs={{7,5},{6,4},{15,13},{14,12},{23,21},{22,20},{31,29},{30,28}} | collective-permute-start | bytes 2211848 | tf_op jit(solution)/shard_map/ppermute | solution.py:377
  214.0 21.7 %collective-permute-start.26 = (f32[72,2560]{1,0:T(8,128)}, f32[72,2560]{1,0:T(8,128)}, u32[]{:S(2)}, u32[]{:S(2)}) collective-permute-start(f32[72,2560]{1,0:T(8,128)} %get-tuple-element.160), channel_id=1, source_target_pairs={{0,2},{1,3},{8,10},{9,11},{16,18},{17,19},{24,26},{25,27}} | collective-permute-start | bytes 2211848 | tf_op jit(solution)/shard_map/ppermute | solution.py:377
  215.5 18.8 %collective-permute-start.24 = (f32[272,640]{1,0:T(8,128)}, f32[272,640]{1,0:T(8,128)}, u32[]{:S(2)}, u32[]{:S(2)}) collective-permute-start(f32[272,640]{1,0:T(8,128)} %collective-permute-done.22.refs_1_), channel_id=1, source_target_pairs={{2,4},{3,5},{4,6},{5,7},{10,12},{11,13},{12,14},{13,15},{18,20},{1... | collective-permute-start | bytes 2088968 | tf_op jit(solution)/shard_map/ppermute | solution.py:339
  220.4 15.3 %collective-permute-start.25 = (f32[272,640]{1,0:T(8,128)}, f32[272,640]{1,0:T(8,128)}, u32[]{:S(2)}, u32[]{:S(2)}) collective-permute-start(f32[272,640]{1,0:T(8,128)} %collective-permute-done.23.refs_6_), channel_id=1, source_target_pairs={{5,3},{4,2},{3,1},{2,0},{13,11},{12,10},{11,9},{10,8},{21,19},{20,... | collective-permute-start | bytes 2088968 | tf_op jit(solution)/shard_map/ppermute | solution.py:339
  235.7 15.9 %collective-permute-start.28 = (f32[272,640]{1,0:T(8,128)}, f32[272,640]{1,0:T(8,128)}, u32[]{:S(2)}, u32[]{:S(2)}) collective-permute-start(f32[272,640]{1,0:T(8,128)} %collective-permute-done.24.refs_3_), channel_id=1, source_target_pairs={{4,6},{5,7},{12,14},{13,15},{20,22},{21,23},{28,30},{29,31}} | collective-permute-start | bytes 2088968 | tf_op jit(solution)/shard_map/ppermute | solution.py:339
  239.4 12.2 %collective-permute-start.29 = (f32[272,640]{1,0:T(8,128)}, f32[272,640]{1,0:T(8,128)}, u32[]{:S(2)}, u32[]{:S(2)}) collective-permute-start(f32[272,640]{1,0:T(8,128)} %collective-permute-done.25.refs_4_), channel_id=1, source_target_pairs={{3,1},{2,0},{11,9},{10,8},{19,17},{18,16},{27,25},{26,24}} | collective-permute-start | bytes 2088968 | tf_op jit(solution)/shard_map/ppermute | solution.py:339
  243.6 17.8 %collective-permute-start.31 = (f32[72,2560]{1,0:T(8,128)}, f32[72,2560]{1,0:T(8,128)}, u32[]{:S(2)}, u32[]{:S(2)}) collective-permute-start(f32[72,2560]{1,0:T(8,128)} %get-tuple-element.157), channel_id=1, source_target_pairs={{7,5},{6,4},{5,3},{4,2},{15,13},{14,12},{13,11},{12,10},{23,21},{2... | collective-permute-start | bytes 2211848 | tf_op jit(solution)/shard_map/ppermute | solution.py:377
  247.0 17.8 %collective-permute-start.30 = (f32[72,2560]{1,0:T(8,128)}, f32[72,2560]{1,0:T(8,128)}, u32[]{:S(2)}, u32[]{:S(2)}) collective-permute-start(f32[72,2560]{1,0:T(8,128)} %get-tuple-element.158), channel_id=1, source_target_pairs={{0,2},{1,3},{2,4},{3,5},{8,10},{9,11},{10,12},{11,13},{16,18},{17,... | collective-permute-start | bytes 2211848 | tf_op jit(solution)/shard_map/ppermute | solution.py:377
  267.4 26.6 %collective-permute-start.33 = (f32[72,2560]{1,0:T(8,128)}, f32[72,2560]{1,0:T(8,128)}, u32[]{:S(2)}, u32[]{:S(2)}) collective-permute-start(f32[72,2560]{1,0:T(8,128)} %get-tuple-element.155), channel_id=1, source_target_pairs={{7,5},{6,4},{5,3},{4,2},{3,1},{2,0},{15,13},{14,12},{13,11},{12,10... | collective-permute-start | bytes 2211848 | tf_op jit(solution)/shard_map/ppermute | solution.py:377
  269.3 11.8 %copy-start.15 = (f32[64,2560]{1,0:T(8,128)S(1)}, f32[64,2560]{1,0:T(8,128)}, u32[]{:S(2)}) copy-start(f32[64,2560]{1,0:T(8,128)} %reduce-scatter.3.cloned.1.call-done) | copy-start | bytes 1966084
  269.4 11.8 %copy-start.16 = (f32[64,2560]{1,0:T(8,128)S(1)}, f32[64,2560]{1,0:T(8,128)}, u32[]{:S(2)}) copy-start(f32[64,2560]{1,0:T(8,128)} %reduce-scatter.5.cloned.1.call-done) | copy-start | bytes 1966084
  269.4 24.7 %collective-permute-start.32 = (f32[72,2560]{1,0:T(8,128)}, f32[72,2560]{1,0:T(8,128)}, u32[]{:S(2)}, u32[]{:S(2)}) collective-permute-start(f32[72,2560]{1,0:T(8,128)} %get-tuple-element.156), channel_id=1, source_target_pairs={{0,2},{1,3},{2,4},{3,5},{4,6},{5,7},{8,10},{9,11},{10,12},{11,13},... | collective-permute-start | bytes 2211848 | tf_op jit(solution)/shard_map/ppermute | solution.py:377
  283.5 5.4 %collective-permute-start.35 = (f32[32,2560]{1,0:T(8,128)}, f32[32,2560]{1,0:T(8,128)S(1)}, u32[]{:S(2)}, u32[]{:S(2)}) collective-permute-start(f32[32,2560]{1,0:T(8,128)} %get-tuple-element.177), channel_id=1, source_target_pairs={{0,1},{1,0},{2,3},{3,2},{4,5},{5,4},{6,7},{7,6},{8,9},{9,8},{10,11... | collective-permute-start | bytes 983048 | tf_op jit(solution)/shard_map/ppermute | solution.py:444
  288.2 3.5 %collective-permute-start.34 = (f32[32,2560]{1,0:T(8,128)}, f32[32,2560]{1,0:T(8,128)}, u32[]{:S(2)}, u32[]{:S(2)}) collective-permute-start(f32[32,2560]{1,0:T(8,128)} %get-tuple-element.179), channel_id=1, source_target_pairs={{0,1},{1,0},{2,3},{3,2},{4,5},{5,4},{6,7},{7,6},{8,9},{9,8},{10,11... | collective-permute-start | bytes 983048 | tf_op jit(solution)/shard_map/ppermute | solution.py:444
  297.6 1.7 collective-permute-start.36
  299.4 0.7 copy-start.17
  (2 other events, 1.4 us)
Sparse Core Ops, SparseCore 0:
  82.5 53.3 reduce-scatter.2
  138.2 56.2 reduce-scatter.4
